TPU v7x, 32 devices: a whole 2x2x4 slice. The times are simulated.
32 devices in a mesh: box: 8 (over z, x), dir: 4 (over y, core).
Axes of the slice: x: 2, y: 2, z: 4, core: 2. Of those that a mesh axis runs over, the one named last changes fastest.
Arguments:
- child_pat: bfloat16 [4096, 2, 8, 2048], P('box', None, None, 'dir'), may hold values from -6 to 6
- interp: bfloat16 [64, 4, 128, 128], P('dir'), may hold values from -0.25 to 0.25
- interp_blocks: int32 [64, 4], P('dir'), may hold values from 0 to 15, as said below
- shift_angle: float32 [8, 8192], P(None, 'dir'), may hold values from -3.140625 to 3.140625
- slot_parent: int32 [512], replicated, may hold values from 0 to 511, each once
- far_list: int32 [512, 189], replicated, may hold values from -1 to 511, as said below
- trans: float32 [2, 343, 8192], P(None, None, 'dir'), may hold values from -0.15625 to 0.15625
Outputs:
- far_field: float32 [512, 2, 8, 8192], P('box', None, None, 'dir')
Inputs may be any that keep to these rules, and one draw needn't show every extreme that they name: `interp_blocks`: entry (j, b) is (j * 16 // 64 + o) modulo 16, for four different o of -2 to 2 in increasing order. `far_list`: row p lists, in increasing order of code(p, q), the occupied parents q whose own parents are neighbours of p's parent (coordinates differ by at most one) and that are not neighbours of p, then -1 to the end; each coordinate of q - p lies within -3 to 3; some row lists 189 partners.
All inputs are finite; a program needn't handle non-finite values.
Results may differ from a plain program's by a relative error of at most 0.0029.
Values may be sent and summed in bfloat16 or wider, within the bound.
No kernel may reach another device: no remote copies, remote signals or barrier semaphores. Data moves between devices by JAX's collectives and lax.ppermute only.
A program may use at most 384 MiB of HBM per device.

v0:
```python
import jax
import jax.numpy as jnp
from jax import lax
from jax.sharding import PartitionSpec as P

G = 8


def padded(value, sides, width):
    for axis, dim in sides:
        devices, length = (lax.axis_size(axis), value.shape[dim])
        up = [(i, (i + 1) % devices) for i in range(devices)]
        down = [(j, i) for i, j in up]
        last = lax.slice_in_dim(value, length - width, length, axis=dim)
        leading = lax.slice_in_dim(value, 0, width, axis=dim)
        before = lax.ppermute(last, axis, up)
        after = lax.ppermute(leading, axis, down)
        value = jnp.concatenate([before, value, after], axis=dim)
    return value


def translate(patterns, table, slot_parent, slot_of, far_list, targets):
    grid_side = G
    count = targets.shape[0]
    columns = patterns.shape[2]
    width = patterns.shape[3]
    parent = slot_parent[targets]
    listed = far_list[parent]
    pos_x = (parent // (grid_side * grid_side))[:, None]
    pos_y = (parent // grid_side % grid_side)[:, None]
    pos_z = (parent % grid_side)[:, None]
    within = jnp.arange(49, dtype=jnp.int32)
    off_y = (within // 7 - 3)[None, :]
    off_z = (within % 7 - 3)[None, :]

    def one_plane(plane, total):
        tgt_x = pos_x + plane - 3
        tgt_y = pos_y + off_y
        tgt_z = pos_z + off_z
        in_grid = (
            (tgt_x >= 0)
            & (tgt_x < grid_side)
            & (tgt_y >= 0)
            & (tgt_y < grid_side)
            & (tgt_z >= 0)
            & (tgt_z < grid_side)
        )
        partner = jnp.where(in_grid, tgt_x * grid_side * grid_side + tgt_y * grid_side + tgt_z, -2)
        hit = jnp.any(listed[:, :, None] == partner[:, None, :], axis=1) & in_grid
        source = slot_of[jnp.where(hit, partner, 0)]
        mask = hit.astype(jnp.float32)[:, :, None, None]
        rows = patterns[source]
        plane_tab = lax.dynamic_slice_in_dim(table, (plane * 49).astype(jnp.int32), 49, 1)
        real_tab = plane_tab[0][None, :, None, :]
        imag_tab = plane_tab[1][None, :, None, :]
        real_rows = rows[:, :, 0].astype(jnp.float32) * mask
        imag_rows = rows[:, :, 1].astype(jnp.float32) * mask
        out_real = jnp.sum(real_tab * real_rows - imag_tab * imag_rows, axis=1)
        out_imag = jnp.sum(real_tab * imag_rows + imag_tab * real_rows, axis=1)
        return total + jnp.stack([out_real, out_imag], axis=1)

    empty = jnp.zeros((count, 2, columns, width), jnp.float32)
    return lax.fori_loop(0, 7, one_plane, empty)


def shards(child_pat, interp, interp_blocks, shift_angle, slot_parent, far_list, trans):
    block_size = interp.shape[2]
    local_in = child_pat.shape[3] // block_size
    total_in = local_in * lax.axis_size("dir")
    out_blocks = interp.shape[0]
    children = child_pat.shape[0]
    columns = child_pat.shape[2]
    extended = padded(child_pat, (("dir", 3),), 2 * block_size)
    row_count = children * 2 * columns
    ext_blocks = local_in + 4
    flat_in = extended.reshape(row_count, ext_blocks * block_size)
    local_index = (interp_blocks - lax.axis_index("dir") * local_in + 2) % total_in
    onehot = (
        local_index[:, :, None] == jnp.arange(ext_blocks, dtype=jnp.int32)[None, None, :]
    ).astype(jnp.bfloat16)
    dense = jnp.einsum("jbl,jbio->lijo", onehot, interp, preferred_element_type=jnp.float32).astype(
        jnp.bfloat16
    )
    dense = dense.reshape(ext_blocks * block_size, out_blocks * block_size)
    upsampled = jnp.dot(flat_in, dense, preferred_element_type=jnp.float32)
    upsampled = upsampled.reshape(children // 8, 8, 2, columns, out_blocks * block_size)
    cosine = jnp.cos(shift_angle)[None, :, None, :]
    sine = jnp.sin(shift_angle)[None, :, None, :]
    real_part = upsampled[:, :, 0]
    imag_part = upsampled[:, :, 1]
    out_real = jnp.sum(cosine * real_part - sine * imag_part, axis=1)
    out_imag = jnp.sum(sine * real_part + cosine * imag_part, axis=1)
    parent_pat = jnp.stack([out_real, out_imag], axis=1).astype(jnp.bfloat16)
    total_parents = slot_parent.shape[0]
    slot_of = (
        jnp.zeros((total_parents,), jnp.int32)
        .at[slot_parent]
        .set(jnp.arange(total_parents, dtype=jnp.int32))
    )
    slots_here = parent_pat.shape[0]
    gathered = lax.all_gather(parent_pat, "box", axis=0, tiled=True)
    targets = lax.axis_index("box") * slots_here + jnp.arange(slots_here, dtype=jnp.int32)
    far_field = translate(gathered, trans, slot_parent, slot_of, far_list, targets)
    return far_field


def solution(mesh):
    in_specs = (
        P("box", None, None, "dir"),
        P("dir", None, None, None),
        P("dir", None),
        P(None, "dir"),
        P(),
        P(),
        P(None, None, "dir"),
    )
    out_specs = P("box", None, None, "dir")
    return jax.shard_map(shards, mesh=mesh, in_specs=in_specs, out_specs=out_specs, check_vma=False)
```

profile of v0, /device:TPU:11, one launch (start us, length us, event | category | flops | bytes accessed | tf_op | source)
XLA Modules:
  0.0 2811.1 jit_solution(11147828640016806503)
XLA Ops:
  28.7 75.6 %collective-permute-done = bf16[512,2,8,256]{3,2,1,0:T(8,128)(2,1)} collective-permute-done((bf16[512,2,8,256]{3,2,1,0:T(8,128)(2,1)}, bf16[512,2,8,256]{3,2,1,0:T(8,128)(2,1)}, u32[]{:S(2)}, u32[]{:S(2)}) %collective-permute-start) | collective-permute-done | bytes 4194336 | tf_op jit(solution)/shard_map/ppermute | solution.py:16
  105.7 14.2 pad_maximum_fusion
  119.9 44.6 %fusion.29 = f32[64,8,2,8,2048]{4,3,2,1,0:T(8,128)} fusion(bf16[64,8,2,8,1024]{4,3,2,1,0:T(8,128)(2,1)} %bitcast.128, bf16[1024,2048,1,1,1]{1,0,2,3,4:T(8,128)(2,1)} %reshape.801), kind=kOutput, calls=%fused_computation.74 | convolution fusion | flops 34359738368 | bytes 88080384 | tf_op jit(solution)/shard_map/dot_general | solution.py:85
  164.4 26.9 subtract_reduce_fusion
  197.9 633.4 %all-gather.2.cloned.1.call-done = bf16[512,2,8,2048]{3,2,1,0:T(8,128)(2,1)} async-done(((bf16[64,2,8,2048]{3,2,1,0:T(8,128)(2,1)}), bf16[512,2,8,2048]{3,2,1,0:T(8,128)(2,1)}) %all-gather.2.cloned.1.call-update) | async-done | bytes 33554448 | tf_op jit(solution)/shard_map/all_gather | solution.py:101
  831.3 1971.3 %while.17 = (s32[]{:T(128)}, f32[64,2,8,2048]{3,2,1,0:T(8,128)}, f32[2,343,2048]{2,0,1:T(2,128)}, s32[64,189]{1,0:T(8,128)S(1)}, s32[64,1]{0,1:T(1,128)S(1)}, /*...) while((s32[]{:T(128)}, f32[64,2,8,2048]{3,2,1,0:T(8,128)}, ...), condition=%wide.region_7.8_spmd.clone.clone, body=%wide.region_3.7_spmd.clone.clone.sunk | while | flops 622099200 | bytes 654970816 | solution.py:63
  833.9 18.9 gather_fusion
  853.3 107.9 %gather_fusion.1 = bf16[3136,2,8,2048]{3,2,1,0:T(8,128)(2,1)} fusion(bf16[512,2,8,2048]{3,2,1,0:T(8,128)(2,1)} %get-tuple-element.510, s32[4096]{0:T(1024)S(1)} %pad_clamp_fusion.7), kind=kCustom, calls=%fused_computation.1.clone.clone.1 | custom fusion | bytes 411054336 | tf_op jit(solution)/shard_map/while/body/eval_jaxpr/gather | solution.py:52
  963.8 137.1 %fusion.49 = (f32[64,8,2048]{2,1,0:T(8,128)}, f32[64,8,2048]{2,1,0:T(8,128)}) fusion(f32[49,2048]{1,0:T(8,128)S(1)} %get-tuple-element.468, f32[64,49]{1,0:T(8,128)S(1)} %copy.57, f32[49,2048]{1,0:T(8,128)S(1)} %get-tuple-element.471, bf16[64,49,2,8,2048]{4,3,2,1,0:T(8,128)(2,1)} %bitcast.123), kind=kLoop, calls=%fused_computation.11.clone.1 | loop fusion | flops 614465536 | bytes 214724864 | tf_op jit(solution)/shard_map/while/body/eval_jaxpr/reduce_sum | solution.py:58
  1110.5 18.9 gather_fusion
  1129.9 118.1 %gather_fusion.1 = bf16[3136,2,8,2048]{3,2,1,0:T(8,128)(2,1)} fusion(bf16[512,2,8,2048]{3,2,1,0:T(8,128)(2,1)} %get-tuple-element.510, s32[4096]{0:T(1024)S(1)} %pad_clamp_fusion.7), kind=kCustom, calls=%fused_computation.1.clone.clone.1 | custom fusion | bytes 411054336 | tf_op jit(solution)/shard_map/while/body/eval_jaxpr/gather | solution.py:52
  1250.6 137.1 %fusion.49 = (f32[64,8,2048]{2,1,0:T(8,128)}, f32[64,8,2048]{2,1,0:T(8,128)}) fusion(f32[49,2048]{1,0:T(8,128)S(1)} %get-tuple-element.468, f32[64,49]{1,0:T(8,128)S(1)} %copy.57, f32[49,2048]{1,0:T(8,128)S(1)} %get-tuple-element.471, bf16[64,49,2,8,2048]{4,3,2,1,0:T(8,128)(2,1)} %bitcast.123), kind=kLoop, calls=%fused_computation.11.clone.1 | loop fusion | flops 614465536 | bytes 214724864 | tf_op jit(solution)/shard_map/while/body/eval_jaxpr/reduce_sum | solution.py:58
  1387.7 9.5 maximum_add_fusion.2
  1399.8 18.9 gather_fusion
  1419.2 109.7 %gather_fusion.1 = bf16[3136,2,8,2048]{3,2,1,0:T(8,128)(2,1)} fusion(bf16[512,2,8,2048]{3,2,1,0:T(8,128)(2,1)} %get-tuple-element.510, s32[4096]{0:T(1024)S(1)} %pad_clamp_fusion.7), kind=kCustom, calls=%fused_computation.1.clone.clone.1 | custom fusion | bytes 411054336 | tf_op jit(solution)/shard_map/while/body/eval_jaxpr/gather | solution.py:52
  1531.4 137.1 %fusion.49 = (f32[64,8,2048]{2,1,0:T(8,128)}, f32[64,8,2048]{2,1,0:T(8,128)}) fusion(f32[49,2048]{1,0:T(8,128)S(1)} %get-tuple-element.468, f32[64,49]{1,0:T(8,128)S(1)} %copy.57, f32[49,2048]{1,0:T(8,128)S(1)} %get-tuple-element.471, bf16[64,49,2,8,2048]{4,3,2,1,0:T(8,128)(2,1)} %bitcast.123), kind=kLoop, calls=%fused_computation.11.clone.1 | loop fusion | flops 614465536 | bytes 214724864 | tf_op jit(solution)/shard_map/while/body/eval_jaxpr/reduce_sum | solution.py:58
  1668.6 9.5 maximum_add_fusion.2
  1680.7 18.9 gather_fusion
  1700.0 115.1 %gather_fusion.1 = bf16[3136,2,8,2048]{3,2,1,0:T(8,128)(2,1)} fusion(bf16[512,2,8,2048]{3,2,1,0:T(8,128)(2,1)} %get-tuple-element.510, s32[4096]{0:T(1024)S(1)} %pad_clamp_fusion.7), kind=kCustom, calls=%fused_computation.1.clone.clone.1 | custom fusion | bytes 411054336 | tf_op jit(solution)/shard_map/while/body/eval_jaxpr/gather | solution.py:52
  1817.7 137.1 %fusion.49 = (f32[64,8,2048]{2,1,0:T(8,128)}, f32[64,8,2048]{2,1,0:T(8,128)}) fusion(f32[49,2048]{1,0:T(8,128)S(1)} %get-tuple-element.468, f32[64,49]{1,0:T(8,128)S(1)} %copy.57, f32[49,2048]{1,0:T(8,128)S(1)} %get-tuple-element.471, bf16[64,49,2,8,2048]{4,3,2,1,0:T(8,128)(2,1)} %bitcast.123), kind=kLoop, calls=%fused_computation.11.clone.1 | loop fusion | flops 614465536 | bytes 214724864 | tf_op jit(solution)/shard_map/while/body/eval_jaxpr/reduce_sum | solution.py:58
  1954.9 9.5 maximum_add_fusion.2
  1966.9 18.9 gather_fusion
  1986.3 110.0 %gather_fusion.1 = bf16[3136,2,8,2048]{3,2,1,0:T(8,128)(2,1)} fusion(bf16[512,2,8,2048]{3,2,1,0:T(8,128)(2,1)} %get-tuple-element.510, s32[4096]{0:T(1024)S(1)} %pad_clamp_fusion.7), kind=kCustom, calls=%fused_computation.1.clone.clone.1 | custom fusion | bytes 411054336 | tf_op jit(solution)/shard_map/while/body/eval_jaxpr/gather | solution.py:52
  2098.9 137.1 %fusion.49 = (f32[64,8,2048]{2,1,0:T(8,128)}, f32[64,8,2048]{2,1,0:T(8,128)}) fusion(f32[49,2048]{1,0:T(8,128)S(1)} %get-tuple-element.468, f32[64,49]{1,0:T(8,128)S(1)} %copy.57, f32[49,2048]{1,0:T(8,128)S(1)} %get-tuple-element.471, bf16[64,49,2,8,2048]{4,3,2,1,0:T(8,128)(2,1)} %bitcast.123), kind=kLoop, calls=%fused_computation.11.clone.1 | loop fusion | flops 614465536 | bytes 214724864 | tf_op jit(solution)/shard_map/while/body/eval_jaxpr/reduce_sum | solution.py:58
  2236.0 9.5 maximum_add_fusion.2
  2248.1 18.9 gather_fusion
  2267.5 120.0 %gather_fusion.1 = bf16[3136,2,8,2048]{3,2,1,0:T(8,128)(2,1)} fusion(bf16[512,2,8,2048]{3,2,1,0:T(8,128)(2,1)} %get-tuple-element.510, s32[4096]{0:T(1024)S(1)} %pad_clamp_fusion.7), kind=kCustom, calls=%fused_computation.1.clone.clone.1 | custom fusion | bytes 411054336 | tf_op jit(solution)/shard_map/while/body/eval_jaxpr/gather | solution.py:52
  2390.1 137.1 %fusion.49 = (f32[64,8,2048]{2,1,0:T(8,128)}, f32[64,8,2048]{2,1,0:T(8,128)}) fusion(f32[49,2048]{1,0:T(8,128)S(1)} %get-tuple-element.468, f32[64,49]{1,0:T(8,128)S(1)} %copy.57, f32[49,2048]{1,0:T(8,128)S(1)} %get-tuple-element.471, bf16[64,49,2,8,2048]{4,3,2,1,0:T(8,128)(2,1)} %bitcast.123), kind=kLoop, calls=%fused_computation.11.clone.1 | loop fusion | flops 614465536 | bytes 214724864 | tf_op jit(solution)/shard_map/while/body/eval_jaxpr/reduce_sum | solution.py:58
  2527.2 9.5 maximum_add_fusion.2
  2539.3 18.9 gather_fusion
  2558.7 94.6 %gather_fusion.1 = bf16[3136,2,8,2048]{3,2,1,0:T(8,128)(2,1)} fusion(bf16[512,2,8,2048]{3,2,1,0:T(8,128)(2,1)} %get-tuple-element.510, s32[4096]{0:T(1024)S(1)} %pad_clamp_fusion.7), kind=kCustom, calls=%fused_computation.1.clone.clone.1 | custom fusion | bytes 411054336 | tf_op jit(solution)/shard_map/while/body/eval_jaxpr/gather | solution.py:52
  2656.0 137.1 %fusion.49 = (f32[64,8,2048]{2,1,0:T(8,128)}, f32[64,8,2048]{2,1,0:T(8,128)}) fusion(f32[49,2048]{1,0:T(8,128)S(1)} %get-tuple-element.468, f32[64,49]{1,0:T(8,128)S(1)} %copy.57, f32[49,2048]{1,0:T(8,128)S(1)} %get-tuple-element.471, bf16[64,49,2,8,2048]{4,3,2,1,0:T(8,128)(2,1)} %bitcast.123), kind=kLoop, calls=%fused_computation.11.clone.1 | loop fusion | flops 614465536 | bytes 214724864 | tf_op jit(solution)/shard_map/while/body/eval_jaxpr/reduce_sum | solution.py:58
  (255 shorter events, 87.2 us)
Async XLA Ops:
  6.5 7.9 copy-start
  6.5 7.8 copy-start.9
  6.5 824.8 %all-gather.2.cloned.1.call-start = ((), (), s32[]{:S(2)}) async-start(), calls=%async_computation | async-start | bytes 37748736 | tf_op jit(solution)/shard_map/all_gather | solution.py:101
  12.6 91.7 %collective-permute-start = (bf16[512,2,8,256]{3,2,1,0:T(8,128)(2,1)}, bf16[512,2,8,256]{3,2,1,0:T(8,128)(2,1)}, u32[]{:S(2)}, u32[]{:S(2)}) collective-permute-start(bf16[512,2,8,256]{3,2,1,0:T(8,128)(2,1)} %get-tuple-element.395), channel_id=1, source_target_pairs={{0,1},{1,2},{2,3},{3,0},{4,5},{5,6},{6,7},{7,4},{8,9},{9,10},{10,1... | collective-permute-start | bytes 12582920 | tf_op jit(solution)/shard_map/ppermute | solution.py:16
  14.4 91.4 %collective-permute-start.1 = (bf16[512,2,8,256]{3,2,1,0:T(8,128)(2,1)}, bf16[512,2,8,256]{3,2,1,0:T(8,128)(2,1)}, u32[]{:S(2)}, u32[]{:S(2)}) collective-permute-start(bf16[512,2,8,256]{3,2,1,0:T(8,128)(2,1)} %get-tuple-element.396), channel_id=1, source_target_pairs={{1,0},{2,1},{3,2},{0,3},{5,4},{6,5},{7,6},{4,7},{9,8},{10,9},{11,1... | collective-permute-start | bytes 12582920 | tf_op jit(solution)/shard_map/ppermute | solution.py:17
  16.5 11.9 copy-start.8
  831.3 21.5 copy-start.2
  1101.0 6.9 copy-start.11
  1107.9 21.4 copy-start.2
  1387.7 9.5 copy-start.3
  1387.7 9.5 copy-start.6
  1387.7 9.5 copy-start.11
  1397.2 21.4 copy-start.2
  1668.6 9.5 copy-start.3
  1668.6 9.5 copy-start.6
  1668.6 9.5 copy-start.11
  1678.1 21.4 copy-start.2
  1954.8 9.5 copy-start.3
  1954.8 9.5 copy-start.6
  1954.9 9.5 copy-start.11
  1964.4 21.4 copy-start.2
  2236.0 9.5 copy-start.3
  2236.0 9.5 copy-start.6
  2236.0 9.5 copy-start.11
  2245.5 21.4 copy-start.2
  2527.2 9.5 copy-start.3
  2527.2 9.5 copy-start.6
  2527.2 9.5 copy-start.11
  2536.7 21.4 copy-start.2
  2793.1 9.5 copy-start.3
  2793.1 9.5 copy-start.6
  2793.1 9.5 copy-start.11
  (19 other events, 28.4 us)
Sparse Core Ops, SparseCore 0:
  193.8 637.4 all-gather.1
where the time goes:
time: 2840 us; the launch traced here: 2810 us
  other arithmetic  1080 us (38%)
  local copies, waits for them, and re-layouts  957 us (34%)
  waiting for transfers between devices  710 us (25%)
  matrix products  46.6 us (2%)
    reduce_sum x7, other arithmetic, one_plane(): out_real = jnp.sum(real_tab * real_rows - imag_tab * imag_rows, axis=1)  960 us
    gather x7, local copies, waits for them, and re-layouts, one_plane(): rows = patterns[source]  775 us
    all_gather x1, waiting for transfers between devices, shards(): gathered = lax.all_gather(parent_pat, 'box', axis=0, tiled=True)  633 us
    gather x21, local copies, waits for them, and re-layouts, one_plane(): source = slot_of[jnp.where(hit, partner, 0)]  134 us
    ppermute x1, waiting for transfers between devices, padded(): before = lax.ppermute(last, axis, up)  75.6 us
    add x7, other arithmetic, one_plane(): return total + jnp.stack([out_real, out_imag], axis=1)  63.7 us
  transfers between devices with their start and end apart: 3, of which 3 were waited for; matrix products, arithmetic and copies ran while one was open for 1% of the time, Pallas kernels for 0%

commit v1 on v0

v1 whole, which is shorter than its diff:
```python
import functools

import jax
import jax.numpy as jnp
import numpy as np
from jax import lax
from jax.experimental import pallas as pl
from jax.experimental.pallas import tpu as pltpu
from jax.sharding import PartitionSpec as P

LANES = 128
G = 8
HALF = G // 2
POINTS = 5
FREQ = 128
MIB = 1024 * 1024


def parent_order():
    octant = np.arange(8)
    grand = np.arange(HALF**3)
    ox, oy, oz = octant // 4, octant // 2 % 2, octant % 2
    gx, gy, gz = grand // HALF**2, grand // HALF % HALF, grand % HALF
    x = 2 * gx[None, :] + ox[:, None]
    y = 2 * gy[None, :] + oy[:, None]
    z = 2 * gz[None, :] + oz[:, None]
    return (x * G * G + y * G + z).reshape(-1).astype(np.int32)


def cover_rows():
    rows = []
    for low, high in ((3, 4), (2, 5)):
        for x in (low, high):
            for y in (low, high):
                for z in (low, high):
                    rows.append((x, y, z))
    seen = np.zeros((G, G, G), bool)
    axis = np.arange(G)
    for x, y, z in rows:
        near = [np.abs(axis - c) <= 1 for c in (x, y, z)]
        reach = [np.abs(axis // 2 - c // 2) <= 1 for c in (x, y, z)]
        cube = [v[0][:, None, None] & v[1][None, :, None] & v[2][None, None, :] for v in (near, reach)]
        seen |= cube[1] & ~cube[0]
    assert seen.all()
    return np.array([(x * G + y) * G + z for x, y, z in rows], np.int32)


def freq_points():
    index = np.arange(POINTS**3)
    return np.stack([index // POINTS**2, index // POINTS % POINTS, index % POINTS], 1)


def grid_points(side, start):
    index = np.arange(side**3)
    return np.stack([index // side**2, index // side % side, index % side], 1) + start


def real_form(matrix):
    return np.block([[matrix.real, -matrix.imag], [matrix.imag, matrix.real]])


def pad_rows(matrix, rows):
    return np.concatenate([matrix, np.zeros((rows - matrix.shape[0], matrix.shape[1]), matrix.dtype)])


def split(matrix):
    high = matrix.astype(jnp.bfloat16)
    low = (matrix - high.astype(np.float64)).astype(jnp.bfloat16)
    return high, low


def forward_matrix():
    phase = np.exp(-2j * np.pi / POINTS * (freq_points() @ grid_points(HALF, 0).T))
    high, low = split(real_form(pad_rows(phase, FREQ)))
    return np.concatenate([high, low], 1)


def inverse_matrix():
    phase = np.exp(2j * np.pi / POINTS * (grid_points(HALF, 0) @ freq_points().T)) / POINTS**3
    phase = pad_rows(phase.T, FREQ).T
    high, low = split(real_form(phase))
    return np.concatenate([high, high, low], 1)


def table_matrix():
    phase = np.exp(2j * np.pi / POINTS * (freq_points() @ grid_points(3, -1).T))
    return real_form(pad_rows(phase, FREQ)).astype(np.float32)


def tap_codes():
    delta = grid_points(3, -1)
    tap = grid_points(3, -1)
    offset = 2 * tap[None, :, :] + delta[:, None, :]
    code = ((offset + 3) * np.array([49, 7, 1])).sum(-1)
    far = np.abs(offset).max(-1) >= 2
    return code.astype(np.int32), far.astype(np.float32)


def table_of(trans, first, width, repeat):
    part = lax.dynamic_slice_in_dim(trans, first, width, 2)
    code, far = tap_codes()
    deltas, taps = code.shape
    rows = jnp.take(part, code.reshape(-1), axis=1).reshape(2, deltas, taps, width)
    rows = rows * far[None, :, :, None]
    matrix = jnp.asarray(table_matrix().reshape(2, FREQ, 2, taps))
    hat = jnp.einsum("cfet,edtk->cdfk", matrix, rows, precision=lax.Precision.HIGHEST)
    real, imag = hat[0], hat[1]
    forms = jnp.stack([real, imag - real, real + imag])
    return jnp.tile(forms, (1, 1, 1, repeat))


def upsample_kernel(offsets, me_ref, own, left, right, interp, cosine, sine, *rest, centers, tiles, roll):
    outs = rest[:tiles]
    weights, held = rest[tiles:]
    blocks_in = own.shape[1] // LANES
    per_center = weights.shape[2] // LANES
    window = weights.shape[1] // LANES
    half = window // 2
    slots = own.shape[0] // LANES
    left_blocks = left.shape[1] // LANES

    @pl.when(pl.program_id(0) == 0)
    def _():
        weights[...] = jnp.zeros_like(weights)
        for index, center in enumerate(centers):
            for j in range(per_center):
                row = center * per_center + j
                for b in range(interp.shape[1]):
                    start = pl.multiple_of(offsets[row, b] * LANES, LANES)
                    weights[index, pl.ds(start, LANES), j * LANES : (j + 1) * LANES] = interp[row, b]

    group = 4
    rows = group * LANES

    def step(i, carry):
        base = pl.multiple_of(i * rows, rows)
        for index, center in enumerate(centers):
            low, high = center - half, center + half + 1
            pieces = []
            if low < 0:
                pieces.append(left[pl.ds(base, rows), (left_blocks + low) * LANES :])
            pieces.append(own[pl.ds(base, rows), max(low, 0) * LANES : min(high, blocks_in) * LANES])
            if high > blocks_in:
                pieces.append(right[pl.ds(base, rows), : (high - blocks_in) * LANES])
            u = jnp.dot(
                jnp.concatenate(pieces, axis=1), weights[index], preferred_element_type=jnp.float32
            )
            u = u.reshape(group, 8, 2, 8, per_center * LANES)
            columns = slice(center * per_center * LANES, (center + 1) * per_center * LANES)
            real = jnp.zeros((group, 8, per_center * LANES), jnp.float32)
            imag = real
            for h in range(8):
                c = cosine[h : h + 1, columns][None]
                s = sine[h : h + 1, columns][None]
                real += c * u[:, h, 0] - s * u[:, h, 1]
                imag += s * u[:, h, 0] + c * u[:, h, 1]
            real = real.reshape(group * 8, per_center * LANES)
            imag = imag.reshape(group * 8, per_center * LANES)
            at = pl.ds(pl.multiple_of(i * group * 8, group * 8), group * 8)
            for j in range(per_center):
                lanes = slice(j * LANES, (j + 1) * LANES)
                held[index * per_center + j, 0, at, :] = real[:, lanes]
                held[index * per_center + j, 1, at, :] = imag[:, lanes]
        return carry

    lax.fori_loop(0, slots // group, step, 0)
    for s in range(tiles):
        tile = lax.rem(me_ref[0] + s, tiles) if roll else s
        for t in range(2):
            for r in range(8):
                outs[s][t, r] = held[tile, t, pl.ds(r, slots, stride=8), :].astype(jnp.bfloat16)


def upsample(own, left, right, interp, offsets, cosine, sine, me, centers, roll):
    rows = own.shape[0]
    slots = rows // LANES
    block = min(16, slots)
    per_center = interp.shape[0] // (own.shape[1] // LANES)
    window = 5
    tiles = len(centers) * per_center
    depth = block * LANES

    def rowwise(array):
        return pl.BlockSpec((depth, array.shape[1]), lambda i: (i, 0))

    whole = pl.BlockSpec(memory_space=pltpu.VMEM)
    smem = pl.BlockSpec(memory_space=pltpu.SMEM)
    return pl.pallas_call(
        functools.partial(upsample_kernel, centers=centers, tiles=tiles, roll=roll),
        grid=(slots // block,),
        in_specs=[smem, smem, rowwise(own), rowwise(left), rowwise(right), whole, whole, whole],
        out_specs=[pl.BlockSpec((2, 8, block, LANES), lambda i: (0, 0, i, 0))] * tiles,
        out_shape=[jax.ShapeDtypeStruct((2, 8, slots, LANES), jnp.bfloat16)] * tiles,
        scratch_shapes=[
            pltpu.VMEM((len(centers), window * LANES, per_center * LANES), jnp.bfloat16),
            pltpu.VMEM((tiles, 2, block * 8, LANES), jnp.float32),
        ],
        compiler_params=pltpu.CompilerParams(vmem_limit_bytes=48 * MIB),
        cost_estimate=pl.CostEstimate(
            flops=2 * rows * window * LANES * tiles * LANES, bytes_accessed=14 * MIB, transcendentals=0
        ),
        name="upsample",
    )(offsets, me, own, left, right, interp, cosine, sine)


def far_kernel(into, back, forward, inverse, table, *rest, count):
    ins = rest[:count]
    outs = rest[count : 2 * count]
    moved, hat, prod, near = rest[2 * count :]
    grand = HALF**3
    slots = ins[0].shape[2]

    for t in range(2):
        columns = [jnp.concatenate([ref[t, r] for ref in ins], axis=0) for r in range(2)]
        rows = jnp.concatenate(columns, axis=1)
        moved[t] = jnp.dot(into[...], rows, preferred_element_type=jnp.float32).astype(jnp.bfloat16)

    for octant in range(8):
        at = slice(octant * grand, (octant + 1) * grand)
        both = jnp.concatenate([moved[0, at], moved[1, at]], axis=0)
        both = jnp.concatenate([both, both], axis=0)
        hat[octant] = jnp.dot(forward[...], both, preferred_element_type=jnp.float32)

    def products(i, carry):
        at = pl.multiple_of(i * 8, 8)
        real_at, imag_at = pl.ds(at, 8), pl.ds(FREQ + at, 8)
        for r in range(2):
            lanes = slice(r * LANES, (r + 1) * LANES)
            real = [hat[s, real_at, lanes] for s in range(8)]
            imag = [hat[s, imag_at, lanes] for s in range(8)]
            total = [a + b for a, b in zip(real, imag)]
            for t in range(8):
                sums = [None] * 3
                for s in range(8):
                    delta = 0
                    for shift in (2, 1, 0):
                        delta = delta * 3 + (s >> shift & 1) - (t >> shift & 1) + 1
                    terms = (
                        table[0, delta, real_at] * total[s],
                        table[1, delta, real_at] * real[s],
                        table[2, delta, real_at] * imag[s],
                    )
                    sums = [b if a is None else a + b for a, b in zip(sums, terms)]
                prod[t, real_at, lanes] = sums[0] - sums[2]
                prod[t, imag_at, lanes] = sums[0] + sums[1]
        return carry

    lax.fori_loop(0, FREQ // 8, products, 0)

    for octant in range(8):
        value = prod[octant]
        high = value.astype(jnp.bfloat16)
        low = (value - high.astype(jnp.float32)).astype(jnp.bfloat16)
        stacked = jnp.concatenate([high, low, high], axis=0)
        result = jnp.dot(inverse[...], stacked, preferred_element_type=jnp.float32)
        at = slice(octant * grand, (octant + 1) * grand)
        near[0, at] = result[:grand].astype(jnp.bfloat16)
        near[1, at] = result[grand:].astype(jnp.bfloat16)

    for t in range(2):
        result = jnp.dot(back[...], near[t], preferred_element_type=jnp.float32).astype(jnp.bfloat16)
        for index, ref in enumerate(outs):
            for r in range(2):
                ref[t, r] = result[index * slots : (index + 1) * slots, r * LANES : (r + 1) * LANES]


def far_field(pieces, into, back, table):
    count = len(pieces)
    _, columns, slots, _ = pieces[0].shape
    parents = into.shape[0]
    whole = pl.BlockSpec(memory_space=pltpu.VMEM)
    piece = pl.BlockSpec((2, 2, slots, LANES), lambda i: (0, i, 0, 0))
    return pl.pallas_call(
        functools.partial(far_kernel, count=count),
        grid=(columns // 2,),
        in_specs=[whole] * 5 + [piece] * count,
        out_specs=[piece] * count,
        out_shape=[jax.ShapeDtypeStruct(pieces[0].shape, jnp.bfloat16)] * count,
        scratch_shapes=[
            pltpu.VMEM((2, parents, 2 * LANES), jnp.bfloat16),
            pltpu.VMEM((8, 2 * FREQ, 2 * LANES), jnp.float32),
            pltpu.VMEM((8, 2 * FREQ, 2 * LANES), jnp.float32),
            pltpu.VMEM((2, parents, 2 * LANES), jnp.bfloat16),
        ],
        compiler_params=pltpu.CompilerParams(vmem_limit_bytes=48 * MIB),
        cost_estimate=pl.CostEstimate(flops=10_000_000_000, bytes_accessed=12 * MIB, transcendentals=0),
        name="far_field",
    )(into, back, jnp.asarray(forward_matrix()), jnp.asarray(inverse_matrix()), table, *pieces)


def finish_kernel(me_ref, *refs, chunks, tiles, first_tile):
    ins = refs[: chunks * tiles]
    out, held = refs[chunks * tiles :]
    slots = ins[0].shape[2]
    for chunk in range(chunks):
        for s in range(tiles):
            tile = lax.rem(me_ref[0] + tiles - s, tiles)
            ref = ins[chunk * tiles + s]
            for t in range(2):
                for r in range(8):
                    held[tile, pl.ds(t * 8 + r, slots, stride=16), :] = ref[t, r].astype(jnp.float32)
        for tile in range(tiles):
            at = first_tile[chunk][tile] * LANES
            out[:, at : at + LANES] = held[tile]


def finish(results, me, first_tile):
    chunks, tiles = len(results), len(results[0])
    slots = results[0][0].shape[2]
    block = min(16, slots)
    width = chunks * tiles * LANES
    return pl.pallas_call(
        functools.partial(finish_kernel, chunks=chunks, tiles=tiles, first_tile=first_tile),
        grid=(slots // block,),
        in_specs=[pl.BlockSpec(memory_space=pltpu.SMEM)]
        + [pl.BlockSpec((2, 8, block, LANES), lambda i: (0, 0, i, 0))] * (chunks * tiles),
        out_specs=pl.BlockSpec((block * 16, width), lambda i: (i, 0)),
        out_shape=jax.ShapeDtypeStruct((slots * 16, width), jnp.float32),
        scratch_shapes=[pltpu.VMEM((tiles, block * 16, LANES), jnp.float32)],
        compiler_params=pltpu.CompilerParams(vmem_limit_bytes=48 * MIB),
        name="finish",
    )(me, *[piece for result in results for piece in result])


def exchange(pieces, axis):
    devices = len(pieces)
    moved = [pieces[0]]
    for s in range(1, devices):
        moved.append(lax.ppermute(pieces[s], axis, [(i, (i + s) % devices) for i in range(devices)]))
    return moved


def shards(child_pat, interp, interp_blocks, shift_angle, slot_parent, far_list, trans):
    boxes = lax.axis_size("box")
    box = lax.axis_index("box")
    directions = lax.axis_size("dir")
    children, _, columns, width_in = child_pat.shape
    local_in = width_in // LANES
    per_center = interp.shape[0] // local_in
    total_in = local_in * directions
    slots = children // 8
    rows = children * 2 * columns
    own = child_pat.reshape(rows, width_in)
    me = box.reshape(1).astype(jnp.int32)

    up = [(i, (i + 1) % directions) for i in range(directions)]
    down = [(j, i) for i, j in up]

    def block_of(index):
        return lax.slice_in_dim(own, index * LANES, (index + 1) * LANES, axis=1)

    before1 = lax.ppermute(block_of(local_in - 1), "dir", up)
    after0 = lax.ppermute(block_of(0), "dir", down)
    before0 = lax.ppermute(block_of(local_in - 2), "dir", up)
    after1 = lax.ppermute(block_of(1), "dir", down)

    centers = jnp.arange(interp.shape[0], dtype=jnp.int32) // per_center + lax.axis_index("dir") * local_in
    offsets = (interp_blocks - centers[:, None] + 2) % total_in
    cosine = jnp.cos(shift_angle)
    sine = jnp.sin(shift_angle)

    pairs = [(i, local_in - 1 - i) for i in reversed(range(local_in // 2))]
    tiles = 2 * per_center
    share = tiles * LANES // boxes
    repeat = max(1, LANES // share)
    assert share * repeat == LANES and columns % (2 * repeat) == 0

    order = parent_order()
    listed = jnp.concatenate([far_list[row] for row in cover_rows()])
    occupied = jnp.any(listed[:, None] == order[None, :], axis=0)
    parent_of = slot_parent.reshape(boxes, slots)
    shifts = jnp.arange(boxes, dtype=jnp.int32)
    arriving = parent_of[(box - shifts) % boxes].reshape(-1)
    leaving = parent_of[(box + shifts) % boxes].reshape(-1)
    into = ((arriving[None, :] == order[:, None]) & occupied[:, None]).astype(jnp.bfloat16)
    back = (leaving[:, None] == order[None, :]).astype(jnp.bfloat16)

    tables = []
    for low, high in pairs:
        at = box * share
        middle = per_center * LANES
        first = jnp.where(at < middle, low * middle + at, high * middle + at - middle)
        tables.append(table_of(trans, first, share, repeat))

    def pieces_of(values):
        if repeat == 1:
            return values
        value = jnp.stack(values).reshape(tiles, 2, columns // repeat, repeat, slots, repeat, share)
        value = value.transpose(0, 5, 1, 2, 4, 3, 6).reshape(boxes, 2, columns // repeat, slots, LANES)
        value = jnp.roll(value, -box, axis=0)
        return [value[s] for s in range(boxes)]

    def tiles_of(values):
        value = jnp.roll(jnp.stack(values)[::-1], box + 1, axis=0)
        value = value.reshape(tiles, repeat, 2, columns // repeat, slots, repeat, share)
        value = value.transpose(4, 2, 3, 5, 0, 1, 6).reshape(slots, 2, columns, 2, per_center * LANES)
        return value.astype(jnp.float32)

    sides = [(before1, after0)]
    sides.append((jnp.concatenate([before0, before1], axis=1), jnp.concatenate([after0, after1], axis=1)))
    results = []
    for index, pair in enumerate(pairs):
        left, right = sides[index]
        patterns = upsample(own, left, right, interp, offsets, cosine, sine, me, pair, repeat == 1)
        gathered = exchange(pieces_of(patterns), "box")
        results.append(gathered)
    results = [far_field(gathered, into, back, table) for gathered, table in zip(results, tables)]
    results = [exchange(result, "box") for result in results]

    if repeat == 1:
        first_tile = [[pair[t // per_center] * per_center + t % per_center for t in range(tiles)] for pair in pairs]
        out = finish(results, me, first_tile)
        return out.reshape(slots, 2, columns, local_in * per_center * LANES)
    parts = [None] * local_in
    for pair, result in zip(pairs, results):
        value = tiles_of(result)
        for side, center in enumerate(pair):
            parts[center] = value[:, :, :, side]
    return jnp.concatenate(parts, axis=-1)


def solution(mesh):
    in_specs = (
        P("box", None, None, "dir"),
        P("dir", None, None, None),
        P("dir", None),
        P(None, "dir"),
        P(),
        P(),
        P(None, None, "dir"),
    )
    out_specs = P("box", None, None, "dir")
    return jax.shard_map(shards, mesh=mesh, in_specs=in_specs, out_specs=out_specs, check_vma=False)
```

time: 2840 us -> 323 us (0.11); the launches traced: 2810 us -> 323 us
  other arithmetic: 1080 us -> 20.5 us
  local copies, waits for them, and re-layouts: 957 us -> 25.3 us
  waiting for transfers between devices: 710 us -> 156 us
  Pallas kernels: 0 us -> 83.6 us
  matrix products: 46.6 us -> 10.7 us
    reduce_sum x8 -> x0, other arithmetic: 987 us -> none  [the longest x7 960 us: one_plane(): out_real = jnp.sum(real_tab * real_rows - imag_tab * imag_rows, axis=1)]
    gather x30 -> x4, local copies, waits for them, and re-layouts: 910 us -> 7.25 us  [the longest x2 6.14 us: table_of(): jnp.take(part, code.reshape(-1), axis=1).reshape(2, deltas, taps, width)]
    all_gather x1 -> x0, waiting for transfers between devices: 633 us -> none  [shards(): gathered = lax.all_gather(parent_pat, 'box', axis=0, tiled=True)]
    pallas_call x0 -> x5, Pallas kernels: none -> 83.6 us  [the longest x2 40.4 us: upsample(): pl.pallas_call(functools.partial(upsample_kernel, centers=centers, tiles=...]
    ppermute x2 -> x32, waiting for transfers between devices: 77 us -> 156 us  [the longest x28 98.3 us: exchange(): lax.ppermute(pieces[s], axis, [(i, (i + s) % devices) for i in range(devi...]
    add x14 -> x1, other arithmetic: 63.8 us -> 0.01 us  [shards(): jnp.arange(interp.shape[0], dtype=jnp.int32) // per_center]
    dot_general x2, matrix products: 46.6 us -> 10.7 us  [table_of(): jnp.einsum('cfet,edtk->cdfk', matrix, rows, precision=lax.Precision.HIGHEST)]
  transfers between devices with their start and end apart: 3 -> 32, of which waited for: 3 -> 15; matrix products, arithmetic and copies ran while one was open for 1% -> 11% of each run, Pallas kernels for 0% -> 18%
where the time goes in v1:
time: 323 us
  waiting for transfers between devices  156 us (48%)
  Pallas kernels  83.6 us (26%)
  starting transfers between devices  26.8 us (8%)
  local copies, waits for them, and re-layouts  25.3 us (8%)
  other arithmetic  20.5 us (6%)
  matrix products  10.7 us (3%)
    ppermute x28, waiting for transfers between devices, exchange(): lax.ppermute(pieces[s], axis, [(i, (i + s) % devices) for i in range(devi...  98.3 us
    ppermute x1, waiting for transfers between devices, shards(): before0 = lax.ppermute(block_of(local_in - 2), 'dir', up)  44.9 us
    pallas_call x2, Pallas kernels, upsample(): pl.pallas_call(functools.partial(upsample_kernel, centers=centers, tiles=...  40.4 us
    pallas_call x2, Pallas kernels, far_field(): pl.pallas_call(functools.partial(far_kernel, count=count), grid=(columns...  37.3 us
    ppermute x28, starting transfers between devices, exchange(): lax.ppermute(pieces[s], axis, [(i, (i + s) % devices) for i in range(devi...  24.3 us
    ppermute x1, waiting for transfers between devices, shards(): before1 = lax.ppermute(block_of(local_in - 1), 'dir', up)  12.6 us
    dot_general x2, matrix products, table_of(): jnp.einsum('cfet,edtk->cdfk', matrix, rows, precision=lax.Precision.HIGHEST)  10.7 us
    unnamed x49, local copies, waits for them, and re-layouts  8.85 us
  transfers between devices with their start and end apart: 32, of which 15 were waited for; matrix products, arithmetic and copies ran while one was open for 11% of the time, Pallas kernels for 18%

profile of v1, /device:TPU:11, one launch (start us, length us, event | category | flops | bytes accessed | tf_op | source)
XLA Modules:
  0.0 323.1 jit_solution(8607041701826625425)
XLA Ops:
  0.0 6.4 %fusion.10 = (bf16[8192,128]{1,0:T(8,128)(2,1)}, bf16[8192,128]{1,0:T(8,128)(2,1)}, bf16[8192,128]{1,0:T(8,128)(2,1)}, bf16[8192,128]{1,0:T(8,128)(2,1)}) fusion(bf16[8192,512]{1,0:T(8,128)(2,1)} %bitcast.32), kind=kLoop, calls=%fused_computation.65 | loop fusion | bytes 16777216 | tf_op jit(solution)/shard_map/slice | solution.py:350
  11.8 3.2 gather_fusion.3
  15.0 2.9 gather_fusion.2
  18.0 5.9 %convolution_bitcast_fusion = f32[2,27,128,128]{3,2,1,0:T(8,128)} fusion(f32[2,128,2,27,1]{1,3,2,4,0:T(8,128)S(1)} %copy-done.16, f32[2,27,27,128]{3,0,2,1:T(2,128)} %bitcast.36, f32[27,27]{1,0:T(8,128)S(1)} %copy-done.17), kind=kOutput, calls=%fused_computation.9 | convolution fusion | flops 573495552 | bytes 4343652 | tf_op jit(solution)/shard_map/cfet,edtk->cdfk/dot_general | solution.py:106
  23.9 4.8 %convolution_bitcast_fusion.1 = f32[2,27,128,128]{3,2,1,0:T(8,128)} fusion(f32[2,128,2,27,1]{1,3,2,4,0:T(8,128)S(1)} %copy-done.16, f32[2,27,27,128]{3,0,2,1:T(2,128)S(1)} %bitcast.35, f32[27,27]{1,0:T(8,128)S(1)} %copy-done.17), kind=kOutput, calls=%fused_computation.10 | convolution fusion | flops 573495552 | bytes 4343652 | tf_op jit(solution)/shard_map/cfet,edtk->cdfk/dot_general | solution.py:106
  30.4 2.6 fusion.11
  33.1 3.0 pad_maximum_fusion.1.table
  37.6 2.7 pad_maximum_fusion.table
  40.6 12.6 %collective-permute-done.left = bf16[8192,128]{1,0:T(8,128)(2,1)S(1)} collective-permute-done((bf16[8192,128]{1,0:T(8,128)(2,1)}, bf16[8192,128]{1,0:T(8,128)(2,1)S(1)}, u32[]{:S(2)}, u32[]{:S(2)}) %collective-permute-start) | collective-permute-done | bytes 2097184 | tf_op jit(solution)/shard_map/ppermute | solution.py:352
  53.2 44.9 %collective-permute-done.16 = bf16[8192,128]{1,0:T(8,128)(2,1)} collective-permute-done((bf16[8192,128]{1,0:T(8,128)(2,1)}, bf16[8192,128]{1,0:T(8,128)(2,1)}, u32[]{:S(2)}, u32[]{:S(2)}) %collective-permute-start.16) | collective-permute-done | bytes 2097184 | tf_op jit(solution)/shard_map/ppermute | solution.py:354
  98.1 4.1 %pad_maximum_fusion.2.left = bf16[8192,256]{1,0:T(8,128)(2,1)} fusion(bf16[8192,128]{1,0:T(8,128)(2,1)S(1)} %collective-permute-done.left, bf16[8192,128]{1,0:T(8,128)(2,1)} %collective-permute-done.16), kind=kLoop, calls=%fused_computation.7 | loop fusion | flops 8388608 | bytes 8388608 | tf_op jit(solution)/shard_map/concatenate | solution.py:400
  102.2 4.9 %pad_maximum_fusion.3.right = bf16[8192,256]{1,0:T(8,128)(2,1)} fusion(bf16[8192,128]{1,0:T(8,128)(2,1)} %collective-permute-done.17, bf16[8192,128]{1,0:T(8,128)(2,1)} %collective-permute-done.1.right), kind=kLoop, calls=%fused_computation.8 | loop fusion | flops 8388608 | bytes 8388608 | tf_op jit(solution)/shard_map/concatenate | solution.py:400
  107.2 20.2 %upsample.3 = (bf16[2,8,64,128]{3,2,1,0:T(8,128)(2,1)S(1)}, bf16[2,8,64,128]{3,2,1,0:T(8,128)(2,1)S(1)}, bf16[2,8,64,128]{3,2,1,0:T(8,128)(2,1)S(1)}, bf16[2,8,6...) custom-call(s32[16,4]{1,0:T(8,128)S(1)} %add_select_fusion.offsets, ...), custom_call_target="tpu_custom_call" | custom-call | flops 10737418240 | bytes 14680064 | tf_op jit(solution)/shard_map/upsample/pallas_call | solution.py:188
  133.9 20.2 %upsample.2 = (bf16[2,8,64,128]{3,2,1,0:T(8,128)(2,1)S(1)}, bf16[2,8,64,128]{3,2,1,0:T(8,128)(2,1)}, bf16[2,8,64,128]{3,2,1,0:T(8,128)(2,1)}, bf16[2,8,64,128]{3...) custom-call(s32[16,4]{1,0:T(8,128)S(1)} %add_select_fusion.offsets, ...), custom_call_target="tpu_custom_call" | custom-call | flops 10737418240 | bytes 14680064 | tf_op jit(solution)/shard_map/upsample/pallas_call | solution.py:188
  158.8 9.6 %collective-permute-done.20.rest_3_ = bf16[2,8,64,128]{3,2,1,0:T(8,128)(2,1)S(1)} collective-permute-done((bf16[2,8,64,128]{3,2,1,0:T(8,128)(2,1)S(1)}, bf16[2,8,64,128]{3,2,1,0:T(8,128)(2,1)S(1)}, u32[]{:S(2)}, u32[]{:S(2)}) %collective-permute-start.20) | collective-permute-done | bytes 262176 | tf_op jit(solution)/shard_map/ppermute | solution.py:329
  169.2 4.9 %collective-permute-done.21.rest_4_ = bf16[2,8,64,128]{3,2,1,0:T(8,128)(2,1)S(1)} collective-permute-done((bf16[2,8,64,128]{3,2,1,0:T(8,128)(2,1)S(1)}, bf16[2,8,64,128]{3,2,1,0:T(8,128)(2,1)S(1)}, u32[]{:S(2)}, u32[]{:S(2)}) %collective-permute-start.21) | collective-permute-done | bytes 262176 | tf_op jit(solution)/shard_map/ppermute | solution.py:329
  176.5 17.0 %collective-permute-done.23.rest_6_ = bf16[2,8,64,128]{3,2,1,0:T(8,128)(2,1)S(1)} collective-permute-done((bf16[2,8,64,128]{3,2,1,0:T(8,128)(2,1)}, bf16[2,8,64,128]{3,2,1,0:T(8,128)(2,1)S(1)}, u32[]{:S(2)}, u32[]{:S(2)}) %collective-permute-start.23) | collective-permute-done | bytes 262176 | tf_op jit(solution)/shard_map/ppermute | solution.py:329
  194.9 2.2 collective-permute-start.8
  200.9 18.7 %far_field.3 = (bf16[2,8,64,128]{3,2,1,0:T(8,128)(2,1)S(1)}, bf16[2,8,64,128]{3,2,1,0:T(8,128)(2,1)S(1)}, bf16[2,8,64,128]{3,2,1,0:T(8,128)(2,1)S(1)}, bf16[2,8,...) custom-call(bf16[512,512]{1,0:T(8,128)(2,1)S(1)} %get-tuple-element., ...), custom_call_target="tpu_custom_call" | custom-call | flops 10000000000 | bytes 12582912 | tf_op jit(solution)/shard_map/far_field/pallas_call | solution.py:273
  221.3 4.2 %collective-permute-start.27 = (bf16[2,8,64,128]{3,2,1,0:T(8,128)(2,1)S(1)}, bf16[2,8,64,128]{3,2,1,0:T(8,128)(2,1)S(1)}, u32[]{:S(2)}, u32[]{:S(2)}) collective-permute-start(bf16[2,8,64,128]{3,2,1,0:T(8,128)(2,1)S(1)} %get-tuple-element.65), channel_id=1, source_target_pairs={{0,12},{4,16},{8,20},{12,24},{16,28},{20,0},{24,4},{28,8},{1,13},{... | collective-permute-start | bytes 786440 | tf_op jit(solution)/shard_map/ppermute | solution.py:329
  226.7 18.5 %far_field.2 = (bf16[2,8,64,128]{3,2,1,0:T(8,128)(2,1)S(1)}, bf16[2,8,64,128]{3,2,1,0:T(8,128)(2,1)S(1)}, bf16[2,8,64,128]{3,2,1,0:T(8,128)(2,1)S(1)}, bf16[2,8,...) custom-call(bf16[512,512]{1,0:T(8,128)(2,1)S(1)} %get-tuple-element., ...), custom_call_target="tpu_custom_call" | custom-call | flops 10000000000 | bytes 12582912 | tf_op jit(solution)/shard_map/far_field/pallas_call | solution.py:273
  245.3 2.1 collective-permute-start.30
  247.7 11.1 %collective-permute-done.27.refs_11_ = bf16[2,8,64,128]{3,2,1,0:T(8,128)(2,1)S(1)} collective-permute-done((bf16[2,8,64,128]{3,2,1,0:T(8,128)(2,1)S(1)}, bf16[2,8,64,128]{3,2,1,0:T(8,128)(2,1)S(1)}, u32[]{:S(2)}, u32[]{:S(2)}) %collective-permute-start.27) | collective-permute-done | bytes 262176 | tf_op jit(solution)/shard_map/ppermute | solution.py:329
  258.8 5.6 %collective-permute-done.28.refs_12_ = bf16[2,8,64,128]{3,2,1,0:T(8,128)(2,1)S(1)} collective-permute-done((bf16[2,8,64,128]{3,2,1,0:T(8,128)(2,1)S(1)}, bf16[2,8,64,128]{3,2,1,0:T(8,128)(2,1)S(1)}, u32[]{:S(2)}, u32[]{:S(2)}) %collective-permute-start.28) | collective-permute-done | bytes 262176 | tf_op jit(solution)/shard_map/ppermute | solution.py:329
  264.4 4.0 %collective-permute-start.12 = (bf16[2,8,64,128]{3,2,1,0:T(8,128)(2,1)S(1)}, bf16[2,8,64,128]{3,2,1,0:T(8,128)(2,1)S(1)}, u32[]{:S(2)}, u32[]{:S(2)}) collective-permute-start(bf16[2,8,64,128]{3,2,1,0:T(8,128)(2,1)S(1)} %get-tuple-element.50), channel_id=1, source_target_pairs={{0,16},{4,20},{8,24},{12,28},{16,0},{20,4},{24,8},{28,12},{1,17},{... | collective-permute-start | bytes 786440 | tf_op jit(solution)/shard_map/ppermute | solution.py:329
  268.4 18.7 %collective-permute-done.30.refs_14_ = bf16[2,8,64,128]{3,2,1,0:T(8,128)(2,1)S(1)} collective-permute-done((bf16[2,8,64,128]{3,2,1,0:T(8,128)(2,1)S(1)}, bf16[2,8,64,128]{3,2,1,0:T(8,128)(2,1)S(1)}, u32[]{:S(2)}, u32[]{:S(2)}) %collective-permute-start.30) | collective-permute-done | bytes 262176 | tf_op jit(solution)/shard_map/ppermute | solution.py:329
  288.9 9.2 %collective-permute-done.11.refs_3_ = bf16[2,8,64,128]{3,2,1,0:T(8,128)(2,1)S(1)} collective-permute-done((bf16[2,8,64,128]{3,2,1,0:T(8,128)(2,1)S(1)}, bf16[2,8,64,128]{3,2,1,0:T(8,128)(2,1)S(1)}, u32[]{:S(2)}, u32[]{:S(2)}) %collective-permute-start.11) | collective-permute-done | bytes 262176 | tf_op jit(solution)/shard_map/ppermute | solution.py:329
  298.1 5.7 %collective-permute-done.12.refs_4_ = bf16[2,8,64,128]{3,2,1,0:T(8,128)(2,1)S(1)} collective-permute-done((bf16[2,8,64,128]{3,2,1,0:T(8,128)(2,1)S(1)}, bf16[2,8,64,128]{3,2,1,0:T(8,128)(2,1)S(1)}, u32[]{:S(2)}, u32[]{:S(2)}) %collective-permute-start.12) | collective-permute-done | bytes 262176 | tf_op jit(solution)/shard_map/ppermute | solution.py:329
  303.8 4.7 %collective-permute-done.13.refs_5_ = bf16[2,8,64,128]{3,2,1,0:T(8,128)(2,1)S(1)} collective-permute-done((bf16[2,8,64,128]{3,2,1,0:T(8,128)(2,1)S(1)}, bf16[2,8,64,128]{3,2,1,0:T(8,128)(2,1)S(1)}, u32[]{:S(2)}, u32[]{:S(2)}) %collective-permute-start.13) | collective-permute-done | bytes 262176 | tf_op jit(solution)/shard_map/ppermute | solution.py:329
  308.5 6.7 %collective-permute-done.14.refs_6_ = bf16[2,8,64,128]{3,2,1,0:T(8,128)(2,1)S(1)} collective-permute-done((bf16[2,8,64,128]{3,2,1,0:T(8,128)(2,1)S(1)}, bf16[2,8,64,128]{3,2,1,0:T(8,128)(2,1)S(1)}, u32[]{:S(2)}, u32[]{:S(2)}) %collective-permute-start.14) | collective-permute-done | bytes 262176 | tf_op jit(solution)/shard_map/ppermute | solution.py:329
  315.2 1.9 collective-permute-done.15.refs_7_
  317.1 6.0 %finish.1 = f32[1024,2048]{1,0:T(8,128)} custom-call(s32[1]{0:T(128)} %bitcast.me_ref, bf16[2,8,64,128]{3,2,1,0:T(8,128)(2,1)S(1)} %get-tuple-element.46.refs_0_, bf16[2,8,64,128]{3,2,1,0:T(8,128)(2,1)S(1)} %collective-permute-done.9.refs_1_, bf16[2,8,64,128]{3,2,1,0:T(8,128)(2,1)S(1)} %collective-permute-done.10.refs_2_, ...), custom_call_target="tpu_custom_call" | custom-call | tf_op jit(solution)/shard_map/finish/pallas_call | solution.py:312
  (114 shorter events, 33.6 us)
Async XLA Ops:
  6.4 46.8 %collective-permute-start = (bf16[8192,128]{1,0:T(8,128)(2,1)}, bf16[8192,128]{1,0:T(8,128)(2,1)S(1)}, u32[]{:S(2)}, u32[]{:S(2)}) collective-permute-start(bf16[8192,128]{1,0:T(8,128)(2,1)} %get-tuple-element.89), channel_id=1, source_target_pairs={{0,1},{1,2},{2,3},{3,0},{4,5},{5,6},{6,7},{7,4},{8,9},{9,10},{10,1... | collective-permute-start | bytes 6291464 | tf_op jit(solution)/shard_map/ppermute | solution.py:352
  8.3 89.9 %collective-permute-start.16 = (bf16[8192,128]{1,0:T(8,128)(2,1)}, bf16[8192,128]{1,0:T(8,128)(2,1)}, u32[]{:S(2)}, u32[]{:S(2)}) collective-permute-start(bf16[8192,128]{1,0:T(8,128)(2,1)} %get-tuple-element.87), channel_id=1, source_target_pairs={{0,1},{1,2},{2,3},{3,0},{4,5},{5,6},{6,7},{7,4},{8,9},{9,10},{10,1... | collective-permute-start | bytes 6291464 | tf_op jit(solution)/shard_map/ppermute | solution.py:354
  8.3 93.9 %collective-permute-start.1 = (bf16[8192,128]{1,0:T(8,128)(2,1)}, bf16[8192,128]{1,0:T(8,128)(2,1)}, u32[]{:S(2)}, u32[]{:S(2)}) collective-permute-start(bf16[8192,128]{1,0:T(8,128)(2,1)} %get-tuple-element.88), channel_id=1, source_target_pairs={{1,0},{2,1},{3,2},{0,3},{5,4},{6,5},{7,6},{4,7},{9,8},{10,9},{11,1... | collective-permute-start | bytes 6291464 | tf_op jit(solution)/shard_map/ppermute | solution.py:353
  8.8 93.4 %collective-permute-start.17 = (bf16[8192,128]{1,0:T(8,128)(2,1)}, bf16[8192,128]{1,0:T(8,128)(2,1)}, u32[]{:S(2)}, u32[]{:S(2)}) collective-permute-start(bf16[8192,128]{1,0:T(8,128)(2,1)} %get-tuple-element.86), channel_id=1, source_target_pairs={{1,0},{2,1},{3,2},{0,3},{5,4},{6,5},{7,6},{4,7},{9,8},{10,9},{11,1... | collective-permute-start | bytes 6291464 | tf_op jit(solution)/shard_map/ppermute | solution.py:355
  128.0 28.2 %collective-permute-start.18 = (bf16[2,8,64,128]{3,2,1,0:T(8,128)(2,1)S(1)}, bf16[2,8,64,128]{3,2,1,0:T(8,128)(2,1)S(1)}, u32[]{:S(2)}, u32[]{:S(2)}) collective-permute-start(bf16[2,8,64,128]{3,2,1,0:T(8,128)(2,1)S(1)} %get-tuple-element.55), channel_id=1, source_target_pairs={{0,4},{4,8},{8,12},{12,16},{16,20},{20,24},{24,28},{28,0},{1,5},{5... | collective-permute-start | bytes 786440 | tf_op jit(solution)/shard_map/ppermute | solution.py:329
  129.3 28.1 %collective-permute-start.19 = (bf16[2,8,64,128]{3,2,1,0:T(8,128)(2,1)S(1)}, bf16[2,8,64,128]{3,2,1,0:T(8,128)(2,1)S(1)}, u32[]{:S(2)}, u32[]{:S(2)}) collective-permute-start(bf16[2,8,64,128]{3,2,1,0:T(8,128)(2,1)S(1)} %get-tuple-element.56), channel_id=1, source_target_pairs={{0,8},{4,12},{8,16},{12,20},{16,24},{20,28},{24,0},{28,4},{1,9},{5... | collective-permute-start | bytes 786440 | tf_op jit(solution)/shard_map/ppermute | solution.py:329
  130.6 37.8 %collective-permute-start.20 = (bf16[2,8,64,128]{3,2,1,0:T(8,128)(2,1)S(1)}, bf16[2,8,64,128]{3,2,1,0:T(8,128)(2,1)S(1)}, u32[]{:S(2)}, u32[]{:S(2)}) collective-permute-start(bf16[2,8,64,128]{3,2,1,0:T(8,128)(2,1)S(1)} %get-tuple-element.57), channel_id=1, source_target_pairs={{0,12},{4,16},{8,20},{12,24},{16,28},{20,0},{24,4},{28,8},{1,13},{... | collective-permute-start | bytes 786440 | tf_op jit(solution)/shard_map/ppermute | solution.py:329
  131.6 42.5 %collective-permute-start.21 = (bf16[2,8,64,128]{3,2,1,0:T(8,128)(2,1)S(1)}, bf16[2,8,64,128]{3,2,1,0:T(8,128)(2,1)S(1)}, u32[]{:S(2)}, u32[]{:S(2)}) collective-permute-start(bf16[2,8,64,128]{3,2,1,0:T(8,128)(2,1)S(1)} %get-tuple-element.58), channel_id=1, source_target_pairs={{0,16},{4,20},{8,24},{12,28},{16,0},{20,4},{24,8},{28,12},{1,17},{... | collective-permute-start | bytes 786440 | tf_op jit(solution)/shard_map/ppermute | solution.py:329
  132.9 43.5 %collective-permute-start.22 = (bf16[2,8,64,128]{3,2,1,0:T(8,128)(2,1)}, bf16[2,8,64,128]{3,2,1,0:T(8,128)(2,1)}, u32[]{:S(2)}, u32[]{:S(2)}) collective-permute-start(bf16[2,8,64,128]{3,2,1,0:T(8,128)(2,1)} %get-tuple-element.59), channel_id=1, source_target_pairs={{0,20},{4,24},{8,28},{12,0},{16,4},{20,8},{24,12},{28,16},{1,21},{... | collective-permute-start | bytes 786440 | tf_op jit(solution)/shard_map/ppermute | solution.py:329
  156.2 37.3 %collective-permute-start.23 = (bf16[2,8,64,128]{3,2,1,0:T(8,128)(2,1)}, bf16[2,8,64,128]{3,2,1,0:T(8,128)(2,1)S(1)}, u32[]{:S(2)}, u32[]{:S(2)}) collective-permute-start(bf16[2,8,64,128]{3,2,1,0:T(8,128)(2,1)} %get-tuple-element.60), channel_id=1, source_target_pairs={{0,24},{4,28},{8,0},{12,4},{16,8},{20,12},{24,16},{28,20},{1,25},{... | collective-permute-start | bytes 786440 | tf_op jit(solution)/shard_map/ppermute | solution.py:329
  157.5 37.4 %collective-permute-start.24 = (bf16[2,8,64,128]{3,2,1,0:T(8,128)(2,1)}, bf16[2,8,64,128]{3,2,1,0:T(8,128)(2,1)S(1)}, u32[]{:S(2)}, u32[]{:S(2)}) collective-permute-start(bf16[2,8,64,128]{3,2,1,0:T(8,128)(2,1)} %get-tuple-element.61), channel_id=1, source_target_pairs={{0,28},{4,0},{8,4},{12,8},{16,12},{20,16},{24,20},{28,24},{1,29},{... | collective-permute-start | bytes 786440 | tf_op jit(solution)/shard_map/ppermute | solution.py:329
  169.2 25.7 %collective-permute-start.2 = (bf16[2,8,64,128]{3,2,1,0:T(8,128)(2,1)}, bf16[2,8,64,128]{3,2,1,0:T(8,128)(2,1)S(1)}, u32[]{:S(2)}, u32[]{:S(2)}) collective-permute-start(bf16[2,8,64,128]{3,2,1,0:T(8,128)(2,1)} %get-tuple-element.39), channel_id=1, source_target_pairs={{0,4},{4,8},{8,12},{12,16},{16,20},{20,24},{24,28},{28,0},{1,5},{5... | collective-permute-start | bytes 786440 | tf_op jit(solution)/shard_map/ppermute | solution.py:329
  174.8 20.1 %collective-permute-start.3 = (bf16[2,8,64,128]{3,2,1,0:T(8,128)(2,1)}, bf16[2,8,64,128]{3,2,1,0:T(8,128)(2,1)S(1)}, u32[]{:S(2)}, u32[]{:S(2)}) collective-permute-start(bf16[2,8,64,128]{3,2,1,0:T(8,128)(2,1)} %get-tuple-element.40), channel_id=1, source_target_pairs={{0,8},{4,12},{8,16},{12,20},{16,24},{20,28},{24,0},{28,4},{1,9},{5... | collective-permute-start | bytes 786440 | tf_op jit(solution)/shard_map/ppermute | solution.py:329
  176.5 43.2 %collective-permute-start.4 = (bf16[2,8,64,128]{3,2,1,0:T(8,128)(2,1)}, bf16[2,8,64,128]{3,2,1,0:T(8,128)(2,1)S(1)}, u32[]{:S(2)}, u32[]{:S(2)}) collective-permute-start(bf16[2,8,64,128]{3,2,1,0:T(8,128)(2,1)} %copy-done.6), channel_id=1, source_target_pairs={{0,12},{4,16},{8,20},{12,24},{16,28},{20,0},{24,4},{28,8},{1,13},{... | collective-permute-start | bytes 786440 | tf_op jit(solution)/shard_map/ppermute | solution.py:329
  193.5 27.3 %collective-permute-start.5 = (bf16[2,8,64,128]{3,2,1,0:T(8,128)(2,1)}, bf16[2,8,64,128]{3,2,1,0:T(8,128)(2,1)S(1)}, u32[]{:S(2)}, u32[]{:S(2)}) collective-permute-start(bf16[2,8,64,128]{3,2,1,0:T(8,128)(2,1)} %copy-done.1), channel_id=1, source_target_pairs={{0,16},{4,20},{8,24},{12,28},{16,0},{20,4},{24,8},{28,12},{1,17},{... | collective-permute-start | bytes 786440 | tf_op jit(solution)/shard_map/ppermute | solution.py:329
  194.9 26.4 %collective-permute-start.6 = (bf16[2,8,64,128]{3,2,1,0:T(8,128)(2,1)S(1)}, bf16[2,8,64,128]{3,2,1,0:T(8,128)(2,1)S(1)}, u32[]{:S(2)}, u32[]{:S(2)}) collective-permute-start(bf16[2,8,64,128]{3,2,1,0:T(8,128)(2,1)S(1)} %get-tuple-element.43), channel_id=1, source_target_pairs={{0,20},{4,24},{8,28},{12,0},{16,4},{20,8},{24,12},{28,16},{1,21},{... | collective-permute-start | bytes 786440 | tf_op jit(solution)/shard_map/ppermute | solution.py:329
  194.9 30.6 %collective-permute-start.7 = (bf16[2,8,64,128]{3,2,1,0:T(8,128)(2,1)S(1)}, bf16[2,8,64,128]{3,2,1,0:T(8,128)(2,1)S(1)}, u32[]{:S(2)}, u32[]{:S(2)}) collective-permute-start(bf16[2,8,64,128]{3,2,1,0:T(8,128)(2,1)S(1)} %get-tuple-element.44), channel_id=1, source_target_pairs={{0,24},{4,28},{8,0},{12,4},{16,8},{20,12},{24,16},{28,20},{1,25},{... | collective-permute-start | bytes 786440 | tf_op jit(solution)/shard_map/ppermute | solution.py:329
  194.9 30.6 %collective-permute-start.8 = (bf16[2,8,64,128]{3,2,1,0:T(8,128)(2,1)S(1)}, bf16[2,8,64,128]{3,2,1,0:T(8,128)(2,1)S(1)}, u32[]{:S(2)}, u32[]{:S(2)}) collective-permute-start(bf16[2,8,64,128]{3,2,1,0:T(8,128)(2,1)S(1)} %get-tuple-element.45), channel_id=1, source_target_pairs={{0,28},{4,0},{8,4},{12,8},{16,12},{20,16},{24,20},{28,24},{1,29},{... | collective-permute-start | bytes 786440 | tf_op jit(solution)/shard_map/ppermute | solution.py:329
  219.7 25.6 %collective-permute-start.25 = (bf16[2,8,64,128]{3,2,1,0:T(8,128)(2,1)S(1)}, bf16[2,8,64,128]{3,2,1,0:T(8,128)(2,1)S(1)}, u32[]{:S(2)}, u32[]{:S(2)}) collective-permute-start(bf16[2,8,64,128]{3,2,1,0:T(8,128)(2,1)S(1)} %get-tuple-element.63), channel_id=1, source_target_pairs={{0,4},{4,8},{8,12},{12,16},{16,20},{20,24},{24,28},{28,0},{1,5},{5... | collective-permute-start | bytes 786440 | tf_op jit(solution)/shard_map/ppermute | solution.py:329
  220.8 26.5 %collective-permute-start.26 = (bf16[2,8,64,128]{3,2,1,0:T(8,128)(2,1)S(1)}, bf16[2,8,64,128]{3,2,1,0:T(8,128)(2,1)S(1)}, u32[]{:S(2)}, u32[]{:S(2)}) collective-permute-start(bf16[2,8,64,128]{3,2,1,0:T(8,128)(2,1)S(1)} %get-tuple-element.64), channel_id=1, source_target_pairs={{0,8},{4,12},{8,16},{12,20},{16,24},{20,28},{24,0},{28,4},{1,9},{5... | collective-permute-start | bytes 786440 | tf_op jit(solution)/shard_map/ppermute | solution.py:329
  221.3 37.5 %collective-permute-start.27 = (bf16[2,8,64,128]{3,2,1,0:T(8,128)(2,1)S(1)}, bf16[2,8,64,128]{3,2,1,0:T(8,128)(2,1)S(1)}, u32[]{:S(2)}, u32[]{:S(2)}) collective-permute-start(bf16[2,8,64,128]{3,2,1,0:T(8,128)(2,1)S(1)} %get-tuple-element.65), channel_id=1, source_target_pairs={{0,12},{4,16},{8,20},{12,24},{16,28},{20,0},{24,4},{28,8},{1,13},{... | collective-permute-start | bytes 786440 | tf_op jit(solution)/shard_map/ppermute | solution.py:329
  225.5 38.9 %collective-permute-start.28 = (bf16[2,8,64,128]{3,2,1,0:T(8,128)(2,1)S(1)}, bf16[2,8,64,128]{3,2,1,0:T(8,128)(2,1)S(1)}, u32[]{:S(2)}, u32[]{:S(2)}) collective-permute-start(bf16[2,8,64,128]{3,2,1,0:T(8,128)(2,1)S(1)} %get-tuple-element.66), channel_id=1, source_target_pairs={{0,16},{4,20},{8,24},{12,28},{16,0},{20,4},{24,8},{28,12},{1,17},{... | collective-permute-start | bytes 786440 | tf_op jit(solution)/shard_map/ppermute | solution.py:329
  225.5 38.9 %collective-permute-start.29 = (bf16[2,8,64,128]{3,2,1,0:T(8,128)(2,1)S(1)}, bf16[2,8,64,128]{3,2,1,0:T(8,128)(2,1)S(1)}, u32[]{:S(2)}, u32[]{:S(2)}) collective-permute-start(bf16[2,8,64,128]{3,2,1,0:T(8,128)(2,1)S(1)} %get-tuple-element.67), channel_id=1, source_target_pairs={{0,20},{4,24},{8,28},{12,0},{16,4},{20,8},{24,12},{28,16},{1,21},{... | collective-permute-start | bytes 786440 | tf_op jit(solution)/shard_map/ppermute | solution.py:329
  245.3 41.7 %collective-permute-start.30 = (bf16[2,8,64,128]{3,2,1,0:T(8,128)(2,1)S(1)}, bf16[2,8,64,128]{3,2,1,0:T(8,128)(2,1)S(1)}, u32[]{:S(2)}, u32[]{:S(2)}) collective-permute-start(bf16[2,8,64,128]{3,2,1,0:T(8,128)(2,1)S(1)} %get-tuple-element.68), channel_id=1, source_target_pairs={{0,24},{4,28},{8,0},{12,4},{16,8},{20,12},{24,16},{28,20},{1,25},{... | collective-permute-start | bytes 786440 | tf_op jit(solution)/shard_map/ppermute | solution.py:329
  247.4 41.5 %collective-permute-start.31 = (bf16[2,8,64,128]{3,2,1,0:T(8,128)(2,1)S(1)}, bf16[2,8,64,128]{3,2,1,0:T(8,128)(2,1)S(1)}, u32[]{:S(2)}, u32[]{:S(2)}) collective-permute-start(bf16[2,8,64,128]{3,2,1,0:T(8,128)(2,1)S(1)} %get-tuple-element.69), channel_id=1, source_target_pairs={{0,28},{4,0},{8,4},{12,8},{16,12},{20,16},{24,20},{28,24},{1,29},{... | collective-permute-start | bytes 786440 | tf_op jit(solution)/shard_map/ppermute | solution.py:329
  258.8 30.1 %collective-permute-start.10 = (bf16[2,8,64,128]{3,2,1,0:T(8,128)(2,1)S(1)}, bf16[2,8,64,128]{3,2,1,0:T(8,128)(2,1)S(1)}, u32[]{:S(2)}, u32[]{:S(2)}) collective-permute-start(bf16[2,8,64,128]{3,2,1,0:T(8,128)(2,1)S(1)} %get-tuple-element.48), channel_id=1, source_target_pairs={{0,8},{4,12},{8,16},{12,20},{16,24},{20,28},{24,0},{28,4},{1,9},{5... | collective-permute-start | bytes 786440 | tf_op jit(solution)/shard_map/ppermute | solution.py:329
  264.4 33.7 %collective-permute-start.11 = (bf16[2,8,64,128]{3,2,1,0:T(8,128)(2,1)S(1)}, bf16[2,8,64,128]{3,2,1,0:T(8,128)(2,1)S(1)}, u32[]{:S(2)}, u32[]{:S(2)}) collective-permute-start(bf16[2,8,64,128]{3,2,1,0:T(8,128)(2,1)S(1)} %get-tuple-element.49), channel_id=1, source_target_pairs={{0,12},{4,16},{8,20},{12,24},{16,28},{20,0},{24,4},{28,8},{1,13},{... | collective-permute-start | bytes 786440 | tf_op jit(solution)/shard_map/ppermute | solution.py:329
  264.4 39.4 %collective-permute-start.12 = (bf16[2,8,64,128]{3,2,1,0:T(8,128)(2,1)S(1)}, bf16[2,8,64,128]{3,2,1,0:T(8,128)(2,1)S(1)}, u32[]{:S(2)}, u32[]{:S(2)}) collective-permute-start(bf16[2,8,64,128]{3,2,1,0:T(8,128)(2,1)S(1)} %get-tuple-element.50), channel_id=1, source_target_pairs={{0,16},{4,20},{8,24},{12,28},{16,0},{20,4},{24,8},{28,12},{1,17},{... | collective-permute-start | bytes 786440 | tf_op jit(solution)/shard_map/ppermute | solution.py:329
  287.0 21.5 %collective-permute-start.13 = (bf16[2,8,64,128]{3,2,1,0:T(8,128)(2,1)S(1)}, bf16[2,8,64,128]{3,2,1,0:T(8,128)(2,1)S(1)}, u32[]{:S(2)}, u32[]{:S(2)}) collective-permute-start(bf16[2,8,64,128]{3,2,1,0:T(8,128)(2,1)S(1)} %get-tuple-element.51), channel_id=1, source_target_pairs={{0,20},{4,24},{8,28},{12,0},{16,4},{20,8},{24,12},{28,16},{1,21},{... | collective-permute-start | bytes 786440 | tf_op jit(solution)/shard_map/ppermute | solution.py:329
  288.9 26.3 %collective-permute-start.14 = (bf16[2,8,64,128]{3,2,1,0:T(8,128)(2,1)S(1)}, bf16[2,8,64,128]{3,2,1,0:T(8,128)(2,1)S(1)}, u32[]{:S(2)}, u32[]{:S(2)}) collective-permute-start(bf16[2,8,64,128]{3,2,1,0:T(8,128)(2,1)S(1)} %get-tuple-element.52), channel_id=1, source_target_pairs={{0,24},{4,28},{8,0},{12,4},{16,8},{20,12},{24,16},{28,20},{1,25},{... | collective-permute-start | bytes 786440 | tf_op jit(solution)/shard_map/ppermute | solution.py:329
  288.9 28.2 %collective-permute-start.15 = (bf16[2,8,64,128]{3,2,1,0:T(8,128)(2,1)S(1)}, bf16[2,8,64,128]{3,2,1,0:T(8,128)(2,1)S(1)}, u32[]{:S(2)}, u32[]{:S(2)}) collective-permute-start(bf16[2,8,64,128]{3,2,1,0:T(8,128)(2,1)S(1)} %get-tuple-element.53), channel_id=1, source_target_pairs={{0,28},{4,0},{8,4},{12,8},{16,12},{20,16},{24,20},{28,24},{1,29},{... | collective-permute-start | bytes 786440 | tf_op jit(solution)/shard_map/ppermute | solution.py:329
  298.1 19.0 %collective-permute-start.9 = (bf16[2,8,64,128]{3,2,1,0:T(8,128)(2,1)S(1)}, bf16[2,8,64,128]{3,2,1,0:T(8,128)(2,1)S(1)}, u32[]{:S(2)}, u32[]{:S(2)}) collective-permute-start(bf16[2,8,64,128]{3,2,1,0:T(8,128)(2,1)S(1)} %get-tuple-element.47), channel_id=1, source_target_pairs={{0,4},{4,8},{8,12},{12,16},{16,20},{20,24},{24,28},{28,0},{1,5},{5... | collective-permute-start | bytes 786440 | tf_op jit(solution)/shard_map/ppermute | solution.py:329
  (24 other events, 284.3 us)

commit v2 on v1

v2 whole, which is shorter than its diff:
```python
import functools

import jax
import jax.numpy as jnp
import numpy as np
from jax import lax
from jax.experimental import pallas as pl
from jax.experimental.pallas import tpu as pltpu
from jax.sharding import PartitionSpec as P

LANES = 128
G = 8
HALF = G // 2
POINTS = 5
FREQ = 128
MIB = 1024 * 1024


def parent_order():
    octant = np.arange(8)
    grand = np.arange(HALF**3)
    ox, oy, oz = octant // 4, octant // 2 % 2, octant % 2
    gx, gy, gz = grand // HALF**2, grand // HALF % HALF, grand % HALF
    x = 2 * gx[None, :] + ox[:, None]
    y = 2 * gy[None, :] + oy[:, None]
    z = 2 * gz[None, :] + oz[:, None]
    return (x * G * G + y * G + z).reshape(-1).astype(np.int32)


def cover_rows():
    rows = []
    for low, high in ((3, 4), (2, 5)):
        for x in (low, high):
            for y in (low, high):
                for z in (low, high):
                    rows.append((x, y, z))
    seen = np.zeros((G, G, G), bool)
    axis = np.arange(G)
    for x, y, z in rows:
        near = [np.abs(axis - c) <= 1 for c in (x, y, z)]
        reach = [np.abs(axis // 2 - c // 2) <= 1 for c in (x, y, z)]
        cube = [v[0][:, None, None] & v[1][None, :, None] & v[2][None, None, :] for v in (near, reach)]
        seen |= cube[1] & ~cube[0]
    assert seen.all()
    return np.array([(x * G + y) * G + z for x, y, z in rows], np.int32)


def freq_points():
    index = np.arange(POINTS**3)
    return np.stack([index // POINTS**2, index // POINTS % POINTS, index % POINTS], 1)


def grid_points(side, start):
    index = np.arange(side**3)
    return np.stack([index // side**2, index // side % side, index % side], 1) + start


def real_form(matrix):
    return np.block([[matrix.real, -matrix.imag], [matrix.imag, matrix.real]])


def pad_rows(matrix, rows):
    return np.concatenate([matrix, np.zeros((rows - matrix.shape[0], matrix.shape[1]), matrix.dtype)])


def split(matrix):
    high = matrix.astype(jnp.bfloat16)
    low = (matrix - high.astype(np.float64)).astype(jnp.bfloat16)
    return high, low


def forward_matrix():
    phase = np.exp(-2j * np.pi / POINTS * (freq_points() @ grid_points(HALF, 0).T))
    high, low = split(real_form(pad_rows(phase, FREQ)))
    return np.concatenate([high, low], 1)


def inverse_matrix():
    phase = np.exp(2j * np.pi / POINTS * (grid_points(HALF, 0) @ freq_points().T)) / POINTS**3
    phase = pad_rows(phase.T, FREQ).T
    high, low = split(real_form(phase))
    return np.concatenate([high, high, low], 1)


TAP_ROWS = 40


def table_matrix():
    phase = np.exp(2j * np.pi / POINTS * (freq_points() @ grid_points(3, -1).T))
    phase = np.concatenate([phase.reshape(-1, 9, 3), np.zeros((POINTS**3, 9, 1))], 2).reshape(-1, 36)
    phase = pad_rows(pad_rows(phase, FREQ).T, TAP_ROWS).T
    high, low = split(real_form(phase))
    return np.concatenate([high, high, low], 1)


def far_codes():
    return (np.abs(grid_points(7, -3)).max(1) >= 2).astype(np.float32)


def table_kernel(place, matrix, far, operator, out, kept, taps):
    codes = operator.shape[0]
    kept[...] = jnp.zeros_like(kept)
    taps[...] = jnp.zeros_like(taps)
    for half in range(2):
        kept[half, :codes] = operator[:, half, :] * far[...]
    for delta, (x, y, z) in enumerate(grid_points(3, 0)):
        for half in range(2):
            for tap in range(9):
                code = (x + 2 * (tap // 3)) * 49 + (y + 2 * (tap % 3)) * 7 + z
                taps[half, 4 * tap : 4 * tap + 4] = kept[half, pl.ds(int(code), 4, stride=2), :]
        value = jnp.concatenate([taps[0], taps[1]], axis=0)
        high = value.astype(jnp.bfloat16)
        low = (value - high.astype(jnp.float32)).astype(jnp.bfloat16)
        stacked = jnp.concatenate([high, low, high], axis=0)
        result = jnp.dot(matrix[...], stacked, preferred_element_type=jnp.float32)
        real, imag = result[:FREQ], result[FREQ:]
        out[0, delta] = real
        out[1, delta] = imag - real
        out[2, delta] = real + imag


def table_of(trans, first, width, repeat):
    trans = jnp.swapaxes(trans, 0, 1)
    codes = trans.shape[0]
    if repeat > 1:
        trans = jnp.tile(lax.dynamic_slice_in_dim(trans, first, width, 2), (1, 1, repeat))
        first = jnp.zeros_like(first)
    whole = pl.BlockSpec(memory_space=pltpu.VMEM)
    return pl.pallas_call(
        table_kernel,
        grid_spec=pltpu.PrefetchScalarGridSpec(
            num_scalar_prefetch=1,
            grid=(1,),
            in_specs=[whole, whole, pl.BlockSpec((codes, 2, LANES), lambda i, place: (0, 0, place[0]))],
            out_specs=pl.BlockSpec((3, 27, FREQ, LANES), lambda i, place: (0, 0, 0, 0)),
            scratch_shapes=[
                pltpu.VMEM((2, (codes // 8 + 2) * 8, LANES), jnp.float32),
                pltpu.VMEM((2, TAP_ROWS, LANES), jnp.float32),
            ],
        ),
        out_shape=jax.ShapeDtypeStruct((3, 27, FREQ, LANES), jnp.float32),
        compiler_params=pltpu.CompilerParams(vmem_limit_bytes=32 * MIB),
        cost_estimate=pl.CostEstimate(flops=1_000_000_000, bytes_accessed=MIB, transcendentals=0),
        name="table",
    )((first // LANES).reshape(1), jnp.asarray(table_matrix()), jnp.asarray(far_codes())[:, None], trans)


def upsample_kernel(places, first, own, halo, interp, cosine, sine, out, weights, held):
    tiles = out.shape[0]
    slots = own.shape[0] // LANES
    lanes = 2 * LANES

    @pl.when(pl.program_id(0) == 0)
    def _():
        weights[...] = jnp.zeros_like(weights)
        for j in range(tiles):
            for b in range(interp.shape[1]):
                start = pl.multiple_of(places[j, b] * LANES, LANES)
                weights[pl.ds(start, LANES), j * LANES : (j + 1) * LANES] = interp[first[0] + j, b]

    group = 4
    rows = group * LANES
    for i in range(slots // group):
        at = slice(i * rows, (i + 1) * rows)
        value = jnp.concatenate([own[at, :], halo[at, :]], axis=1)
        for n in range(tiles // 2):
            columns = slice(n * lanes, (n + 1) * lanes)
            u = jnp.dot(value, weights[:, columns], preferred_element_type=jnp.float32)
            u = u.reshape(group, 8, 2, 8, lanes)
            real = imag = None
            for h in range(8):
                c = cosine[h : h + 1, columns][None]
                s = sine[h : h + 1, columns][None]
                x = c * u[:, h, 0] - s * u[:, h, 1]
                y = s * u[:, h, 0] + c * u[:, h, 1]
                real, imag = (x, y) if h == 0 else (real + x, imag + y)
            kept = slice(i * group * 8, (i + 1) * group * 8)
            for t, part in enumerate((real, imag)):
                part = part.reshape(group * 8, lanes)
                held[2 * n, t, kept, :] = part[:, :LANES]
                held[2 * n + 1, t, kept, :] = part[:, LANES:]
    for tile in range(tiles):
        for t in range(2):
            for r in range(8):
                out[tile, t, r] = held[tile, t, pl.ds(r, slots, stride=8), :].astype(jnp.bfloat16)


def upsample(own, halo, interp, places, first, cosine, sine, begin, cost):
    rows = halo.shape[0]
    slots = rows // LANES
    block = min(16, slots)
    steps = slots // block
    tiles = places.shape[0]
    depth = block * LANES
    width = own.shape[1] + halo.shape[1]
    whole = pl.BlockSpec(memory_space=pltpu.VMEM)
    smem = pl.BlockSpec(memory_space=pltpu.SMEM)
    return pl.pallas_call(
        upsample_kernel,
        grid=(steps,),
        in_specs=[
            smem,
            smem,
            pl.BlockSpec((depth, own.shape[1]), lambda i: (begin // block + i, 0)),
            pl.BlockSpec((depth, halo.shape[1]), lambda i: (i, 0)),
            whole,
            whole,
            whole,
        ],
        out_specs=pl.BlockSpec((tiles, 2, 8, block, LANES), lambda i: (0, 0, 0, i, 0)),
        out_shape=jax.ShapeDtypeStruct((tiles, 2, 8, slots, LANES), jnp.bfloat16),
        scratch_shapes=[
            pltpu.VMEM((width, tiles * LANES), jnp.bfloat16),
            pltpu.VMEM((tiles, 2, block * 8, LANES), jnp.float32),
        ],
        compiler_params=pltpu.CompilerParams(vmem_limit_bytes=48 * MIB),
        cost_estimate=pl.CostEstimate(flops=cost, bytes_accessed=rows, transcendentals=0),
        name="upsample",
    )(places, first, own, halo, interp, cosine, sine)


def far_kernel(into, back, forward, inverse, table, *rest, count):
    ins = rest[:count]
    outs = rest[count:-4]
    moved, hat, prod, near = rest[-4:]
    grand = HALF**3
    boxes = ins[0].shape[0]
    slots = outs[0].shape[3]

    for t in range(2):
        columns = [
            jnp.concatenate([ref[box, t, r] for box in range(boxes) for ref in ins], axis=0) for r in range(2)
        ]
        rows = jnp.concatenate(columns, axis=1)
        moved[t] = jnp.dot(into[...], rows, preferred_element_type=jnp.float32).astype(jnp.bfloat16)

    for octant in range(8):
        at = slice(octant * grand, (octant + 1) * grand)
        both = jnp.concatenate([moved[0, at], moved[1, at]], axis=0)
        both = jnp.concatenate([both, both], axis=0)
        hat[octant] = jnp.dot(forward[...], both, preferred_element_type=jnp.float32)

    def products(i, carry):
        at = pl.multiple_of(i * 8, 8)
        real_at, imag_at = pl.ds(at, 8), pl.ds(FREQ + at, 8)
        for r in range(2):
            lanes = slice(r * LANES, (r + 1) * LANES)
            real = [hat[s, real_at, lanes] for s in range(8)]
            imag = [hat[s, imag_at, lanes] for s in range(8)]
            total = [a + b for a, b in zip(real, imag)]
            for t in range(8):
                sums = [None] * 3
                for s in range(8):
                    delta = 0
                    for shift in (2, 1, 0):
                        delta = delta * 3 + (s >> shift & 1) - (t >> shift & 1) + 1
                    terms = (
                        table[0, delta, real_at] * total[s],
                        table[1, delta, real_at] * real[s],
                        table[2, delta, real_at] * imag[s],
                    )
                    sums = [b if a is None else a + b for a, b in zip(sums, terms)]
                prod[t, real_at, lanes] = sums[0] - sums[2]
                prod[t, imag_at, lanes] = sums[0] + sums[1]
        return carry

    lax.fori_loop(0, FREQ // 8, products, 0)

    for octant in range(8):
        value = prod[octant]
        high = value.astype(jnp.bfloat16)
        low = (value - high.astype(jnp.float32)).astype(jnp.bfloat16)
        stacked = jnp.concatenate([high, low, high], axis=0)
        result = jnp.dot(inverse[...], stacked, preferred_element_type=jnp.float32)
        at = slice(octant * grand, (octant + 1) * grand)
        near[0, at] = result[:grand].astype(jnp.bfloat16)
        near[1, at] = result[grand:].astype(jnp.bfloat16)

    for t in range(2):
        result = jnp.dot(back[...], near[t], preferred_element_type=jnp.float32).astype(jnp.bfloat16)
        for box in range(boxes):
            ref, index = (outs[box], 0) if len(outs) > 1 else (outs[0], box)
            for r in range(2):
                ref[index, t, r] = result[box * slots : (box + 1) * slots, r * LANES : (r + 1) * LANES]


def far_field(parts, into, back, table, apart):
    boxes, _, columns, _, _ = parts[0].shape
    slots = sum(part.shape[3] for part in parts)
    parents = into.shape[0]
    whole = pl.BlockSpec(memory_space=pltpu.VMEM)

    def columnwise(boxes, rows):
        return pl.BlockSpec((boxes, 2, 2, rows, LANES), lambda i: (0, 0, i, 0, 0))

    results, each = (boxes, 1) if apart else (1, boxes)
    return pl.pallas_call(
        functools.partial(far_kernel, count=len(parts)),
        grid=(columns // 2,),
        in_specs=[whole] * 5 + [columnwise(boxes, part.shape[3]) for part in parts],
        out_specs=[columnwise(each, slots)] * results,
        out_shape=[jax.ShapeDtypeStruct((each, 2, columns, slots, LANES), jnp.bfloat16)] * results,
        scratch_shapes=[
            pltpu.VMEM((2, parents, 2 * LANES), jnp.bfloat16),
            pltpu.VMEM((8, 2 * FREQ, 2 * LANES), jnp.float32),
            pltpu.VMEM((8, 2 * FREQ, 2 * LANES), jnp.float32),
            pltpu.VMEM((2, parents, 2 * LANES), jnp.bfloat16),
        ],
        compiler_params=pltpu.CompilerParams(vmem_limit_bytes=48 * MIB),
        cost_estimate=pl.CostEstimate(flops=20_000_000_000, bytes_accessed=12 * MIB, transcendentals=0),
        name="far_field",
    )(into, back, jnp.asarray(forward_matrix()), jnp.asarray(inverse_matrix()), table, *parts)


def finish_kernel(side, me, *rest, tiles):
    ins = rest[:tiles]
    out, held = rest[-2:]
    slots = ins[0].shape[3]
    for s in range(tiles):
        tile = lax.rem(me[0] + tiles - s, tiles)
        for t in range(2):
            for r in range(8):
                held[tile, pl.ds(t * 8 + r, slots, stride=16), :] = ins[s][0, t, r].astype(jnp.float32)
    for tile in range(tiles):
        out[:, tile * LANES : (tile + 1) * LANES] = held[tile]


def finish(results, whole, side, me, width):
    tiles = len(results)
    _, _, _, slots, _ = results[0].shape
    block = min(16, slots)
    kept = [] if whole is None else [whole]
    return pl.pallas_call(
        functools.partial(finish_kernel, tiles=tiles),
        grid_spec=pltpu.PrefetchScalarGridSpec(
            num_scalar_prefetch=2,
            grid=(slots // block,),
            in_specs=[pl.BlockSpec((1, 2, 8, block, LANES), lambda i, *_: (0, 0, 0, i, 0))] * tiles
            + [pl.BlockSpec(memory_space=pl.ANY)] * len(kept),
            out_specs=pl.BlockSpec((block * 16, tiles * LANES), lambda i, side, me: (i, side[0])),
            scratch_shapes=[pltpu.VMEM((tiles, block * 16, LANES), jnp.float32)],
        ),
        out_shape=jax.ShapeDtypeStruct((slots * 16, width), jnp.float32),
        input_output_aliases={2 + tiles: 0} if kept else {},
        compiler_params=pltpu.CompilerParams(vmem_limit_bytes=48 * MIB),
        name="finish",
    )(side, me, *results, *kept)


def exchange(value):
    return lax.all_to_all(value, "box", 0, 0, tiled=True)


def send_apart(pieces):
    devices = len(pieces)
    moved = list(pieces)
    for s in sorted(range(1, devices), key=lambda s: abs(s - devices // 2)):
        moved[s] = lax.ppermute(pieces[s], "box", [(i, (i + s) % devices) for i in range(devices)])
    return moved


def after(value, *others):
    return lax.optimization_barrier((value, *others))[0]


def shards(child_pat, interp, interp_blocks, shift_angle, slot_parent, far_list, trans):
    boxes = lax.axis_size("box")
    box = lax.axis_index("box").astype(jnp.int32)
    directions = lax.axis_size("dir")
    here = lax.axis_index("dir").astype(jnp.int32)
    children, _, columns, width_in = child_pat.shape
    local_in = width_in // LANES
    per_center = interp.shape[0] // local_in
    total_in = local_in * directions
    slots = children // 8
    rows = children * 2 * columns
    own = child_pat.reshape(rows, width_in)
    edge = 2 * LANES

    tiles = interp.shape[0] // 2
    width = tiles * LANES
    share = width // boxes
    repeat = max(1, LANES // share)
    apart = repeat == 1
    assert local_in == 4 and directions % 2 == 0
    assert share * repeat == LANES and columns % (2 * repeat) == 0

    odd = here % 2
    inner = [(i, i + 1 - 2 * (i % 2)) for i in range(directions)]
    outer = [(i, (i + 2 * (i % 2) - 1) % directions) for i in range(directions)]
    sides = [1 - odd, odd]
    def send_edge(source, step, begin, size):
        start = (begin * LANES, sides[step] * (width_in - edge))
        send = lax.dynamic_slice(source, start, (size * LANES, edge))
        return send, lax.ppermute(send, "dir", (inner, outer)[step])

    half = slots // 2
    quarter = half // 2
    send, inner_halo = send_edge(own, 0, 0, slots)
    _, outer_first = send_edge(after(own, send), 1, 0, quarter)

    centers = jnp.arange(interp.shape[0], dtype=jnp.int32) // per_center
    window = (interp_blocks - (centers + here * local_in)[:, None] + 2) % total_in + centers[:, None] - 2

    def places_for(side):
        block = lax.dynamic_slice_in_dim(window, side * tiles, tiles, 0)
        return jnp.where(block < 0, block + local_in + 2, block)

    def pieces_of(value):
        if apart:
            return value
        slots = value.shape[3]
        value = value.reshape(tiles, 2, columns // repeat, repeat, slots, repeat, share)
        return value.transpose(0, 5, 1, 2, 4, 3, 6).reshape(boxes, 2, columns // repeat, slots, LANES)

    def tiles_of(value):
        value = value.reshape(tiles, repeat, 2, columns // repeat, slots, repeat, share)
        return value.transpose(4, 2, 3, 5, 0, 1, 6).reshape(slots, 2, columns, width).astype(jnp.float32)

    def patterns(step, halo, begin, cost):
        angle = lax.dynamic_slice_in_dim(shift_angle, sides[step] * width, width, 1)
        first = (sides[step] * tiles).reshape(1)
        cosine, sine = jnp.cos(angle), jnp.sin(angle)
        return upsample(own, halo, interp, places_for(sides[step]), first, cosine, sine, begin, cost)

    def give_back(pieces):
        return send_apart(pieces) if apart else [exchange(pieces[0])]

    value = patterns(0, inner_halo, 0, 1)
    value, outer_first = lax.optimization_barrier((value, outer_first))
    first = exchange(pieces_of(value))
    _, outer_second = send_edge(after(own, value), 1, quarter, half - quarter)

    operator, slot_parent, far_list, _ = lax.optimization_barrier((trans, slot_parent, far_list, value))
    tables = [table_of(operator, side * width + box * share, share, repeat) for side in sides]
    order = parent_order()
    listed = jnp.concatenate([far_list[row] for row in cover_rows()])
    occupied = jnp.any(listed[:, None] == order[None, :], axis=0)
    into = ((slot_parent[None, :] == order[:, None]) & occupied[:, None]).astype(jnp.bfloat16)
    leaving = slot_parent.reshape(boxes, slots)
    if apart:
        leaving = leaving[(box + jnp.arange(boxes, dtype=jnp.int32)) % boxes]
    back = (leaving.reshape(-1)[:, None] == order[None, :]).astype(jnp.bfloat16)

    _, outer_last = send_edge(after(own, *tables), 1, half, slots - half)
    halo = jnp.concatenate([outer_first, outer_second], axis=0)
    value = patterns(1, after(halo, into, back, *tables), 0, 12_000_000_000)
    second = exchange(pieces_of(value))
    pieces = far_field([after(first, value)], into, back, tables[0], apart)
    value = patterns(1, after(outer_last, pieces[0], second), half, 12_000_000_000)
    third = exchange(pieces_of(value))
    pieces = [after(piece, third) for piece in pieces]
    results = [give_back(pieces)]
    pieces = far_field([second, third], into, back, tables[1], apart)
    results.append(give_back(pieces))

    out = None
    if apart:
        for result, side in zip(results, sides):
            out = finish(result, out, side.reshape(1), box.reshape(1), 2 * width)
        return out.reshape(slots, 2, columns, 2 * width)
    first, second = (tiles_of(result[0]) for result in results)
    ordered = [jnp.where(odd == 1, first, second), jnp.where(odd == 1, second, first)]
    return jnp.concatenate(ordered, axis=-1)


def solution(mesh):
    in_specs = (
        P("box", None, None, "dir"),
        P("dir", None, None, None),
        P("dir", None),
        P(None, "dir"),
        P(),
        P(),
        P(None, None, "dir"),
    )
    out_specs = P("box", None, None, "dir")
    return jax.shard_map(shards, mesh=mesh, in_specs=in_specs, out_specs=out_specs, check_vma=False)
```

time: 323 us -> 257 us (0.80)
  waiting for transfers between devices: 156 us -> 70.7 us
  blocking collectives: 0 us -> 27.7 us
  other arithmetic: 20.5 us -> 5.64 us
  local copies, waits for them, and re-layouts: 25.3 us -> 37 us
  matrix products: 10.7 us -> 0 us
  starting transfers between devices: 26.8 us -> 30.7 us
    ppermute x32 -> x18, waiting for transfers between devices: 156 us -> 70.6 us  [the longest x14 59.7 us: send_apart(): lax.ppermute(pieces[s], 'box', [(i, (i + s) % devices) for i in range(dev...]
    all_to_all x0 -> x1, blocking collectives: none -> 27.7 us  [exchange(): return lax.all_to_all(value, 'box', 0, 0, tiled=True)]
    all_to_all x0 -> x2, starting transfers between devices: none -> 12.1 us  [exchange(): return lax.all_to_all(value, 'box', 0, 0, tiled=True)]
    dot_general x2 -> x0, matrix products: 10.7 us -> none  [table_of(): jnp.einsum('cfet,edtk->cdfk', matrix, rows, precision=lax.Precision.HIGHEST)]
    unnamed x49 -> x87, local copies, waits for them, and re-layouts: 8.85 us -> 19 us
    dynamic_slice x1 -> x4, local copies, waits for them, and re-layouts: 1.16 us -> 11.3 us  [send_edge(): send = lax.dynamic_slice(source, start, (size * LANES, edge))]
    ppermute x32 -> x18, starting transfers between devices: 26.8 us -> 18.5 us  [the longest x14 14.9 us: send_apart(): lax.ppermute(pieces[s], 'box', [(i, (i + s) % devices) for i in range(dev...]
    concatenate x2 -> x1, other arithmetic: 9.01 us -> 1.68 us  [shards(): halo = jnp.concatenate([outer_first, outer_second], axis=0)]
  transfers between devices with their start and end apart: 32 -> 20, of which waited for: 15 -> 12; matrix products, arithmetic and copies ran while one was open for 11% -> 7% of each run, Pallas kernels for 18% -> 28%
where the time goes in v2:
time: 257 us; the launch traced here: 256 us
  Pallas kernels  84.4 us (33%)
  waiting for transfers between devices  70.7 us (28%)
  local copies, waits for them, and re-layouts  37 us (14%)
  starting transfers between devices  30.7 us (12%)
  blocking collectives  27.7 us (11%)
  other arithmetic  5.64 us (2%)
    ppermute x14, waiting for transfers between devices, send_apart(): lax.ppermute(pieces[s], 'box', [(i, (i + s) % devices) for i in range(dev...  59.7 us
    pallas_call x2, Pallas kernels, far_field(): pl.pallas_call(functools.partial(far_kernel, count=len(parts)), grid=(col...  37.1 us
    pallas_call x3, Pallas kernels, upsample(): pl.pallas_call(upsample_kernel, grid=(steps,), in_specs=[smem, smem, pl.B...  36.9 us
    all_to_all x1, blocking collectives, exchange(): return lax.all_to_all(value, 'box', 0, 0, tiled=True)  27.7 us
    unnamed x87, local copies, waits for them, and re-layouts  19 us
    ppermute x14, starting transfers between devices, send_apart(): lax.ppermute(pieces[s], 'box', [(i, (i + s) % devices) for i in range(dev...  14.9 us
    all_to_all x2, starting transfers between devices, exchange(): return lax.all_to_all(value, 'box', 0, 0, tiled=True)  12.1 us
    dynamic_slice x4, local copies, waits for them, and re-layouts, send_edge(): send = lax.dynamic_slice(source, start, (size * LANES, edge))  11.3 us
  transfers between devices with their start and end apart: 20, of which 12 were waited for; matrix products, arithmetic and copies ran while one was open for 7% of the time, Pallas kernels for 28%

profile of v2, /device:TPU:11, one launch (start us, length us, event | category | flops | bytes accessed | tf_op | source)
XLA Modules:
  0.0 256.3 jit_solution(13049681980907319424)
XLA Ops:
  0.0 4.6 %constant_dynamic-slice_fusion.1 = bf16[8192,256]{1,0:T(8,128)(2,1)} fusion(bf16[8192,512]{1,0:T(8,128)(2,1)} %bitcast.16, s32[]{:T(128)S(6)} %select_n.92), kind=kLoop, calls=%fused_computation.40 | loop fusion | bytes 8388612 | tf_op jit(solution)/shard_map/dynamic_slice | solution.py:394
  9.4 3.0 %collective-permute-done.halo = bf16[8192,256]{1,0:T(8,128)(2,1)} collective-permute-done((bf16[8192,256]{1,0:T(8,128)(2,1)}, bf16[8192,256]{1,0:T(8,128)(2,1)}, u32[]{:S(2)}, u32[]{:S(2)}) %collective-permute-start) | collective-permute-done | bytes 4194336 | tf_op jit(solution)/shard_map/ppermute | solution.py:395
  12.4 17.7 %upsample.3 = bf16[8,2,8,64,128]{4,3,2,1,0:T(8,128)(2,1)} custom-call(s32[8,4]{1,0:T(8,128)S(1)} %get-tuple-element.96.places, s32[1]{0:T(128)} %bitcast.2.first, bf16[8192,512]{1,0:T(8,128)(2,1)} %bitcast.18, bf16[8192,256]{1,0:T(8,128)(2,1)} %collective-permute-done.halo, bf16[16,4,128,128]{3,2,1,0:T(8,128)(2,1)S(1)} %copy-done.3, ...), custom_call_target="tpu_custom_call" | custom-call | flops 1 | bytes 8192 | tf_op jit(solution)/shard_map/upsample/pallas_call | solution.py:198
  31.6 5.8 %all-to-all-start.1 = ((bf16[8,2,8,64,128]{4,3,2,1,0:T(8,128)(2,1)}), bf16[8,2,8,64,128]{4,3,2,1,0:T(8,128)(2,1)S(1)}, u32[]{:S(2)}, u32[]{:S(2)}) async-start(bf16[8,2,8,64,128]{4,3,2,1,0:T(8,128)(2,1)} %upsample.3), calls=%async_computation.1 | async-start | bytes 4194304 | tf_op jit(solution)/shard_map/all_to_all | solution.py:351
  39.3 1.9 gather_fusion
  42.6 2.3 constant_dynamic-slice_fusion.3
  44.9 1.7 collective-permute-start.2
  46.6 2.6 %copy-done = f32[2,343,2048]{2,0,1:T(2,128)S(1)} copy-done((f32[2,343,2048]{2,0,1:T(2,128)S(1)}, f32[2,343,2048]{2,0,1:T(2,128)}, u32[]{:S(2)}) %copy-start) | copy-done | bytes 5619736
  53.2 1.7 table.2
  55.0 2.4 copy-done.1
  57.4 3.1 %constant_dynamic-slice_fusion.2 = bf16[4096,256]{1,0:T(8,128)(2,1)} fusion(bf16[8192,512]{1,0:T(8,128)(2,1)} %bitcast.20, s32[]{:T(128)S(6)} %select_n.94), kind=kLoop, calls=%fused_computation.46 | loop fusion | bytes 4194308 | tf_op jit(solution)/shard_map/dynamic_slice | solution.py:394
  64.5 6.5 %collective-permute-done.2 = bf16[2048,256]{1,0:T(8,128)(2,1)} collective-permute-done((bf16[2048,256]{1,0:T(8,128)(2,1)}, bf16[2048,256]{1,0:T(8,128)(2,1)}, u32[]{:S(2)}, u32[]{:S(2)}) %collective-permute-start.2) | collective-permute-done | bytes 1048608 | tf_op jit(solution)/shard_map/ppermute | solution.py:395
  70.9 1.7 pad_maximum_fusion.halo
  72.6 9.4 %upsample.4 = bf16[8,2,8,32,128]{4,3,2,1,0:T(8,128)(2,1)S(1)} custom-call(s32[8,4]{1,0:T(8,128)S(1)} %copy-done.16, s32[1]{0:T(128)} %bitcast.7.first, bf16[8192,512]{1,0:T(8,128)(2,1)} %bitcast.21, bf16[4096,256]{1,0:T(8,128)(2,1)S(1)} %pad_maximum_fusion.halo, bf16[16,4,128,128]{3,2,1,0:T(8,128)(2,1)S(1)} %copy-done.4, f32[8,1024]{1,0:T(8,128)S(1)} %copy-done.15, ...), custom_call_target="tpu_custom_call" | custom-call | flops 12000000000 | bytes 4096 | tf_op jit(solution)/shard_map/upsample/pallas_call | solution.py:198
  83.1 6.3 %all-to-all-start = ((bf16[8,2,8,32,128]{4,3,2,1,0:T(8,128)(2,1)}), bf16[8,2,8,32,128]{4,3,2,1,0:T(8,128)(2,1)S(1)}, u32[]{:S(2)}, u32[]{:S(2)}) async-start(bf16[8,2,8,32,128]{4,3,2,1,0:T(8,128)(2,1)} %copy-done.6), calls=%async_computation | async-start | bytes 2097152 | tf_op jit(solution)/shard_map/all_to_all | solution.py:351
  93.3 18.5 %far_field.2 = (bf16[1,2,8,64,128]{4,3,2,1,0:T(8,128)(2,1)S(1)}, bf16[1,2,8,64,128]{4,3,2,1,0:T(8,128)(2,1)S(1)}, bf16[1,2,8,64,128]{4,3,2,1,0:T(8,128)(2,1)S(1)...) custom-call(bf16[512,512]{1,0:T(8,128)(2,1)S(1)} %copy-done.13, ...), custom_call_target="tpu_custom_call" | custom-call | flops 20000000000 | bytes 12582912 | tf_op jit(solution)/shard_map/far_field/pallas_call | solution.py:297
  118.4 9.8 %upsample.5 = bf16[8,2,8,32,128]{4,3,2,1,0:T(8,128)(2,1)S(1)} custom-call(s32[8,4]{1,0:T(8,128)S(1)} %copy-done.16, s32[1]{0:T(128)} %bitcast.7.first, bf16[8192,512]{1,0:T(8,128)(2,1)} %bitcast.22, bf16[4096,256]{1,0:T(8,128)(2,1)} %collective-permute-done.3.halo, bf16[16,4,128,128]{3,2,1,0:T(8,128)(2,1)S(1)} %copy-done.5, f32[8,1024]{1,0:T(8,128)S(1)} %copy-done.15, ...), custom_call_target="tpu_custom_call" | custom-call | flops 12000000000 | bytes 4096 | tf_op jit(solution)/shard_map/upsample/pallas_call | solution.py:198
  128.2 27.7 %all_to_all.15.rest_1_ = bf16[8,2,8,32,128]{4,3,2,1,0:T(8,128)(2,1)S(1)} all-to-all(bf16[8,2,8,32,128]{4,3,2,1,0:T(8,128)(2,1)S(1)} %upsample.5), channel_id=1, replica_groups=mesh['box'=8,'dir'=4] {'box'}, dimensions={0} | all-to-all | bytes 2097152 | tf_op jit(solution)/shard_map/all_to_all | solution.py:351
  155.9 2.2 collective-permute-start.11
  159.0 2.6 %collective-permute-start.13 = (bf16[1,2,8,64,128]{4,3,2,1,0:T(8,128)(2,1)S(1)}, bf16[1,2,8,64,128]{4,3,2,1,0:T(8,128)(2,1)S(1)}, u32[]{:S(2)}, u32[]{:S(2)}) collective-permute-start(bf16[1,2,8,64,128]{4,3,2,1,0:T(8,128)(2,1)S(1)} %copy-done.26), channel_id=1, source_target_pairs={{0,12},{4,16},{8,20},{12,24},{16,28},{20,0},{24,4},{28,8},{1,13},{... | collective-permute-start | bytes 786440 | tf_op jit(solution)/shard_map/ppermute | solution.py:358
  161.6 18.6 %far_field.3 = (bf16[1,2,8,64,128]{4,3,2,1,0:T(8,128)(2,1)S(1)}, bf16[1,2,8,64,128]{4,3,2,1,0:T(8,128)(2,1)S(1)}, bf16[1,2,8,64,128]{4,3,2,1,0:T(8,128)(2,1)S(1)...) custom-call(bf16[512,512]{1,0:T(8,128)(2,1)S(1)} %copy-done.14, ...), custom_call_target="tpu_custom_call" | custom-call | flops 20000000000 | bytes 12582912 | tf_op jit(solution)/shard_map/far_field/pallas_call | solution.py:297
  180.3 1.7 collective-permute-start.15
  182.0 2.0 collective-permute-start.16
  184.3 2.1 collective-permute-start.4
  186.3 14.9 %collective-permute-done.14.rest_4_ = bf16[1,2,8,64,128]{4,3,2,1,0:T(8,128)(2,1)S(1)} collective-permute-done((bf16[1,2,8,64,128]{4,3,2,1,0:T(8,128)(2,1)S(1)}, bf16[1,2,8,64,128]{4,3,2,1,0:T(8,128)(2,1)S(1)}, u32[]{:S(2)}, u32[]{:S(2)}) %collective-permute-start.14) | collective-permute-done | bytes 262176 | tf_op jit(solution)/shard_map/ppermute | solution.py:358
  201.2 2.7 %collective-permute-done.15.rest_5_ = bf16[1,2,8,64,128]{4,3,2,1,0:T(8,128)(2,1)S(1)} collective-permute-done((bf16[1,2,8,64,128]{4,3,2,1,0:T(8,128)(2,1)S(1)}, bf16[1,2,8,64,128]{4,3,2,1,0:T(8,128)(2,1)S(1)}, u32[]{:S(2)}, u32[]{:S(2)}) %collective-permute-start.15) | collective-permute-done | bytes 262176 | tf_op jit(solution)/shard_map/ppermute | solution.py:358
  203.9 20.5 %collective-permute-done.16.rest_6_ = bf16[1,2,8,64,128]{4,3,2,1,0:T(8,128)(2,1)S(1)} collective-permute-done((bf16[1,2,8,64,128]{4,3,2,1,0:T(8,128)(2,1)S(1)}, bf16[1,2,8,64,128]{4,3,2,1,0:T(8,128)(2,1)S(1)}, u32[]{:S(2)}, u32[]{:S(2)}) %collective-permute-start.16) | collective-permute-done | bytes 262176 | tf_op jit(solution)/shard_map/ppermute | solution.py:358
  224.9 3.1 %collective-permute-start.10 = (bf16[1,2,8,64,128]{4,3,2,1,0:T(8,128)(2,1)S(1)}, bf16[1,2,8,64,128]{4,3,2,1,0:T(8,128)(2,1)S(1)}, u32[]{:S(2)}, u32[]{:S(2)}) collective-permute-start(bf16[1,2,8,64,128]{4,3,2,1,0:T(8,128)(2,1)S(1)} %get-tuple-element.59), channel_id=1, source_target_pairs={{0,28},{4,0},{8,4},{12,8},{16,12},{20,16},{24,20},{28,24},{1,29},{... | collective-permute-start | bytes 786440 | tf_op jit(solution)/shard_map/ppermute | solution.py:358
  228.0 3.5 %finish.2.rest_8_ = f32[1024,2048]{1,0:T(8,128)} custom-call(s32[1]{0:T(128)} %bitcast.9.side, s32[1]{0:T(128)} %bitcast.1.me, bf16[1,2,8,64,128]{4,3,2,1,0:T(8,128)(2,1)S(1)} %get-tuple-element.60.rest_0_, bf16[1,2,8,64,128]{4,3,2,1,0:T(8,128)(2,1)S(1)} %collective-permute-done.11.rest_1_, bf16[1,2,8,64,128]{4,3,2,1,0:T(8,128)(2,1)S(1)} %collective-permute-done.12.rest_2_, ...), custom_call_target="tpu_custom_call" | custom-call | tf_op jit(solution)/shard_map/finish/pallas_call | solution.py:333
  231.6 15.9 %collective-permute-done.7.rest_4_ = bf16[1,2,8,64,128]{4,3,2,1,0:T(8,128)(2,1)S(1)} collective-permute-done((bf16[1,2,8,64,128]{4,3,2,1,0:T(8,128)(2,1)S(1)}, bf16[1,2,8,64,128]{4,3,2,1,0:T(8,128)(2,1)S(1)}, u32[]{:S(2)}, u32[]{:S(2)}) %collective-permute-start.7) | collective-permute-done | bytes 262176 | tf_op jit(solution)/shard_map/ppermute | solution.py:358
  247.5 5.1 %collective-permute-done.9.rest_6_ = bf16[1,2,8,64,128]{4,3,2,1,0:T(8,128)(2,1)S(1)} collective-permute-done((bf16[1,2,8,64,128]{4,3,2,1,0:T(8,128)(2,1)S(1)}, bf16[1,2,8,64,128]{4,3,2,1,0:T(8,128)(2,1)S(1)}, u32[]{:S(2)}, u32[]{:S(2)}) %collective-permute-start.9) | collective-permute-done | bytes 262176 | tf_op jit(solution)/shard_map/ppermute | solution.py:358
  252.7 3.5 %finish.3 = f32[1024,2048]{1,0:T(8,128)} custom-call(s32[1]{0:T(128)} %bitcast.side, s32[1]{0:T(128)} %bitcast.1.me, bf16[1,2,8,64,128]{4,3,2,1,0:T(8,128)(2,1)S(1)} %get-tuple-element.52.rest_0_, bf16[1,2,8,64,128]{4,3,2,1,0:T(8,128)(2,1)S(1)} %collective-permute-done.4.rest_1_, ...), custom_call_target="tpu_custom_call", output_to_operand_aliasing={{}: (10, {})} | custom-call | tf_op jit(solution)/shard_map/finish/pallas_call | solution.py:333
  (124 shorter events, 31.0 us)
Async XLA Ops:
  4.6 7.8 %collective-permute-start = (bf16[8192,256]{1,0:T(8,128)(2,1)}, bf16[8192,256]{1,0:T(8,128)(2,1)}, u32[]{:S(2)}, u32[]{:S(2)}) collective-permute-start(bf16[8192,256]{1,0:T(8,128)(2,1)} %constant_dynamic-slice_fusion.1), channel_id=1, source_target_pairs={{0,1},{1,0},{2,3},{3,2},{4,5},{5,4},{6,7},{7,6},{8,9},{9,8},{10,11... | collective-permute-start | bytes 12582920 | tf_op jit(solution)/shard_map/ppermute | solution.py:395
  6.6 24.9 %collective-permute-start.1 = (bf16[2048,256]{1,0:T(8,128)(2,1)S(1)}, bf16[2048,256]{1,0:T(8,128)(2,1)}, u32[]{:S(2)}, u32[]{:S(2)}) collective-permute-start(bf16[2048,256]{1,0:T(8,128)(2,1)S(1)} %constant_dynamic-slice_fusion), channel_id=1, source_target_pairs={{0,3},{1,2},{2,1},{3,0},{4,7},{5,6},{6,5},{7,4},{8,11},{9,10},{10,... | collective-permute-start | bytes 3145736 | tf_op jit(solution)/shard_map/ppermute | solution.py:395
  31.6 21.1 %slice-start = ((s8[5619712]{0:T(1024)(128)(4,1)}), s8[1425408]{0:T(1024)(128)(4,1)S(1)}, s32[]{:S(2)}) async-start(s8[5619712]{0:T(1024)(128)(4,1)} %bitcast.13), calls=%async_computation.3 | async-start | bytes 2850816
  31.6 51.5 %all-to-all-start.1 = ((bf16[8,2,8,64,128]{4,3,2,1,0:T(8,128)(2,1)}), bf16[8,2,8,64,128]{4,3,2,1,0:T(8,128)(2,1)S(1)}, u32[]{:S(2)}, u32[]{:S(2)}) async-start(bf16[8,2,8,64,128]{4,3,2,1,0:T(8,128)(2,1)} %upsample.3), calls=%async_computation.1 | async-start | bytes 4194304 | tf_op jit(solution)/shard_map/all_to_all | solution.py:351
  44.9 26.1 %collective-permute-start.2 = (bf16[2048,256]{1,0:T(8,128)(2,1)}, bf16[2048,256]{1,0:T(8,128)(2,1)}, u32[]{:S(2)}, u32[]{:S(2)}) collective-permute-start(bf16[2048,256]{1,0:T(8,128)(2,1)} %constant_dynamic-slice_fusion.3), channel_id=1, source_target_pairs={{0,3},{1,2},{2,1},{3,0},{4,7},{5,6},{6,5},{7,4},{8,11},{9,10},{10,... | collective-permute-start | bytes 3145736 | tf_op jit(solution)/shard_map/ppermute | solution.py:395
  60.5 56.2 %collective-permute-start.3 = (bf16[4096,256]{1,0:T(8,128)(2,1)}, bf16[4096,256]{1,0:T(8,128)(2,1)}, u32[]{:S(2)}, u32[]{:S(2)}) collective-permute-start(bf16[4096,256]{1,0:T(8,128)(2,1)} %constant_dynamic-slice_fusion.2), channel_id=1, source_target_pairs={{0,3},{1,2},{2,1},{3,0},{4,7},{5,6},{6,5},{7,4},{8,11},{9,10},{10,... | collective-permute-start | bytes 6291464 | tf_op jit(solution)/shard_map/ppermute | solution.py:395
  83.1 33.7 %all-to-all-start = ((bf16[8,2,8,32,128]{4,3,2,1,0:T(8,128)(2,1)}), bf16[8,2,8,32,128]{4,3,2,1,0:T(8,128)(2,1)S(1)}, u32[]{:S(2)}, u32[]{:S(2)}) async-start(bf16[8,2,8,32,128]{4,3,2,1,0:T(8,128)(2,1)} %copy-done.6), calls=%async_computation | async-start | bytes 2097152 | tf_op jit(solution)/shard_map/all_to_all | solution.py:351
  118.3 37.5 %copy-start.30 = (bf16[1,2,8,64,128]{4,3,2,1,0:T(8,128)(2,1)S(1)}, bf16[1,2,8,64,128]{4,3,2,1,0:T(8,128)(2,1)}, u32[]{:S(2)}) copy-start(bf16[1,2,8,64,128]{4,3,2,1,0:T(8,128)(2,1)} %copy-done.29) | copy-start | bytes 786436
  118.3 39.7 %copy-start.28 = (bf16[1,2,8,64,128]{4,3,2,1,0:T(8,128)(2,1)S(1)}, bf16[1,2,8,64,128]{4,3,2,1,0:T(8,128)(2,1)}, u32[]{:S(2)}) copy-start(bf16[1,2,8,64,128]{4,3,2,1,0:T(8,128)(2,1)} %copy-done.27) | copy-start | bytes 786436
  118.3 40.7 %copy-start.26 = (bf16[1,2,8,64,128]{4,3,2,1,0:T(8,128)(2,1)S(1)}, bf16[1,2,8,64,128]{4,3,2,1,0:T(8,128)(2,1)}, u32[]{:S(2)}) copy-start(bf16[1,2,8,64,128]{4,3,2,1,0:T(8,128)(2,1)} %copy-done.25) | copy-start | bytes 786436
  118.3 43.3 %copy-start.24 = (bf16[1,2,8,64,128]{4,3,2,1,0:T(8,128)(2,1)S(1)}, bf16[1,2,8,64,128]{4,3,2,1,0:T(8,128)(2,1)}, u32[]{:S(2)}) copy-start(bf16[1,2,8,64,128]{4,3,2,1,0:T(8,128)(2,1)} %copy-done.23) | copy-start | bytes 786436
  118.4 43.3 %copy-start.12 = (bf16[512,512]{1,0:T(8,128)(2,1)S(1)}, bf16[512,512]{1,0:T(8,128)(2,1)}, u32[]{:S(2)}) copy-start(bf16[512,512]{1,0:T(8,128)(2,1)} %get-tuple-element.97.back) | copy-start | bytes 1572868
  118.4 43.3 %copy-start.14 = (bf16[512,512]{1,0:T(8,128)(2,1)S(1)}, bf16[512,512]{1,0:T(8,128)(2,1)}, u32[]{:S(2)}) copy-start(bf16[512,512]{1,0:T(8,128)(2,1)} %get-tuple-element.98.into) | copy-start | bytes 1572868
  118.4 43.3 %copy-start.32 = (bf16[128,768]{1,0:T(8,128)(2,1)S(1)}, bf16[128,768]{1,0:T(8,128)(2,1)}, u32[]{:S(2)}) copy-start(bf16[128,768]{1,0:T(8,128)(2,1)} %constant.130.clone.inverse) | copy-start | bytes 589828
  118.4 43.3 %copy-start.34 = (bf16[256,256]{1,0:T(8,128)(2,1)S(1)}, bf16[256,256]{1,0:T(8,128)(2,1)}, u32[]{:S(2)}) copy-start(bf16[256,256]{1,0:T(8,128)(2,1)} %constant.129.clone.forward) | copy-start | bytes 393220
  155.9 24.4 %copy-start.22 = (bf16[1,2,8,64,128]{4,3,2,1,0:T(8,128)(2,1)S(1)}, bf16[1,2,8,64,128]{4,3,2,1,0:T(8,128)(2,1)}, u32[]{:S(2)}) copy-start(bf16[1,2,8,64,128]{4,3,2,1,0:T(8,128)(2,1)} %copy-done.21) | copy-start | bytes 786436
  155.9 26.1 %copy-start.20 = (bf16[1,2,8,64,128]{4,3,2,1,0:T(8,128)(2,1)S(1)}, bf16[1,2,8,64,128]{4,3,2,1,0:T(8,128)(2,1)}, u32[]{:S(2)}) copy-start(bf16[1,2,8,64,128]{4,3,2,1,0:T(8,128)(2,1)} %copy-done.19) | copy-start | bytes 786436
  155.9 28.1 %copy-start.18 = (bf16[1,2,8,64,128]{4,3,2,1,0:T(8,128)(2,1)S(1)}, bf16[1,2,8,64,128]{4,3,2,1,0:T(8,128)(2,1)}, u32[]{:S(2)}) copy-start(bf16[1,2,8,64,128]{4,3,2,1,0:T(8,128)(2,1)} %copy-done.17) | copy-start | bytes 786436
  155.9 26.1 %collective-permute-start.11 = (bf16[1,2,8,64,128]{4,3,2,1,0:T(8,128)(2,1)S(1)}, bf16[1,2,8,64,128]{4,3,2,1,0:T(8,128)(2,1)S(1)}, u32[]{:S(2)}, u32[]{:S(2)}) collective-permute-start(bf16[1,2,8,64,128]{4,3,2,1,0:T(8,128)(2,1)S(1)} %copy-done.30), channel_id=1, source_target_pairs={{0,4},{4,8},{8,12},{12,16},{16,20},{20,24},{24,28},{28,0},{1,5},{5... | collective-permute-start | bytes 786440 | tf_op jit(solution)/shard_map/ppermute | solution.py:358
  158.0 25.9 %collective-permute-start.12 = (bf16[1,2,8,64,128]{4,3,2,1,0:T(8,128)(2,1)S(1)}, bf16[1,2,8,64,128]{4,3,2,1,0:T(8,128)(2,1)S(1)}, u32[]{:S(2)}, u32[]{:S(2)}) collective-permute-start(bf16[1,2,8,64,128]{4,3,2,1,0:T(8,128)(2,1)S(1)} %copy-done.28), channel_id=1, source_target_pairs={{0,8},{4,12},{8,16},{12,20},{16,24},{20,28},{24,0},{28,4},{1,9},{5... | collective-permute-start | bytes 786440 | tf_op jit(solution)/shard_map/ppermute | solution.py:358
  159.0 25.3 %collective-permute-start.13 = (bf16[1,2,8,64,128]{4,3,2,1,0:T(8,128)(2,1)S(1)}, bf16[1,2,8,64,128]{4,3,2,1,0:T(8,128)(2,1)S(1)}, u32[]{:S(2)}, u32[]{:S(2)}) collective-permute-start(bf16[1,2,8,64,128]{4,3,2,1,0:T(8,128)(2,1)S(1)} %copy-done.26), channel_id=1, source_target_pairs={{0,12},{4,16},{8,20},{12,24},{16,28},{20,0},{24,4},{28,8},{1,13},{... | collective-permute-start | bytes 786440 | tf_op jit(solution)/shard_map/ppermute | solution.py:358
  161.6 39.6 %collective-permute-start.14 = (bf16[1,2,8,64,128]{4,3,2,1,0:T(8,128)(2,1)S(1)}, bf16[1,2,8,64,128]{4,3,2,1,0:T(8,128)(2,1)S(1)}, u32[]{:S(2)}, u32[]{:S(2)}) collective-permute-start(bf16[1,2,8,64,128]{4,3,2,1,0:T(8,128)(2,1)S(1)} %copy-done.24), channel_id=1, source_target_pairs={{0,16},{4,20},{8,24},{12,28},{16,0},{20,4},{24,8},{28,12},{1,17},{... | collective-permute-start | bytes 786440 | tf_op jit(solution)/shard_map/ppermute | solution.py:358
  180.3 23.6 %collective-permute-start.15 = (bf16[1,2,8,64,128]{4,3,2,1,0:T(8,128)(2,1)S(1)}, bf16[1,2,8,64,128]{4,3,2,1,0:T(8,128)(2,1)S(1)}, u32[]{:S(2)}, u32[]{:S(2)}) collective-permute-start(bf16[1,2,8,64,128]{4,3,2,1,0:T(8,128)(2,1)S(1)} %copy-done.22), channel_id=1, source_target_pairs={{0,20},{4,24},{8,28},{12,0},{16,4},{20,8},{24,12},{28,16},{1,21},{... | collective-permute-start | bytes 786440 | tf_op jit(solution)/shard_map/ppermute | solution.py:358
  182.0 42.4 %collective-permute-start.16 = (bf16[1,2,8,64,128]{4,3,2,1,0:T(8,128)(2,1)S(1)}, bf16[1,2,8,64,128]{4,3,2,1,0:T(8,128)(2,1)S(1)}, u32[]{:S(2)}, u32[]{:S(2)}) collective-permute-start(bf16[1,2,8,64,128]{4,3,2,1,0:T(8,128)(2,1)S(1)} %copy-done.20), channel_id=1, source_target_pairs={{0,24},{4,28},{8,0},{12,4},{16,8},{20,12},{24,16},{28,20},{1,25},{... | collective-permute-start | bytes 786440 | tf_op jit(solution)/shard_map/ppermute | solution.py:358
  184.0 40.6 %collective-permute-start.17 = (bf16[1,2,8,64,128]{4,3,2,1,0:T(8,128)(2,1)S(1)}, bf16[1,2,8,64,128]{4,3,2,1,0:T(8,128)(2,1)S(1)}, u32[]{:S(2)}, u32[]{:S(2)}) collective-permute-start(bf16[1,2,8,64,128]{4,3,2,1,0:T(8,128)(2,1)S(1)} %copy-done.18), channel_id=1, source_target_pairs={{0,28},{4,0},{8,4},{12,8},{16,12},{20,16},{24,20},{28,24},{1,29},{... | collective-permute-start | bytes 786440 | tf_op jit(solution)/shard_map/ppermute | solution.py:358
  184.3 40.3 %collective-permute-start.4 = (bf16[1,2,8,64,128]{4,3,2,1,0:T(8,128)(2,1)S(1)}, bf16[1,2,8,64,128]{4,3,2,1,0:T(8,128)(2,1)S(1)}, u32[]{:S(2)}, u32[]{:S(2)}) collective-permute-start(bf16[1,2,8,64,128]{4,3,2,1,0:T(8,128)(2,1)S(1)} %get-tuple-element.53), channel_id=1, source_target_pairs={{0,4},{4,8},{8,12},{12,16},{16,20},{20,24},{24,28},{28,0},{1,5},{5... | collective-permute-start | bytes 786440 | tf_op jit(solution)/shard_map/ppermute | solution.py:358
  201.2 23.7 %collective-permute-start.5 = (bf16[1,2,8,64,128]{4,3,2,1,0:T(8,128)(2,1)S(1)}, bf16[1,2,8,64,128]{4,3,2,1,0:T(8,128)(2,1)S(1)}, u32[]{:S(2)}, u32[]{:S(2)}) collective-permute-start(bf16[1,2,8,64,128]{4,3,2,1,0:T(8,128)(2,1)S(1)} %get-tuple-element.54), channel_id=1, source_target_pairs={{0,8},{4,12},{8,16},{12,20},{16,24},{20,28},{24,0},{28,4},{1,9},{5... | collective-permute-start | bytes 786440 | tf_op jit(solution)/shard_map/ppermute | solution.py:358
  203.9 27.7 %collective-permute-start.6 = (bf16[1,2,8,64,128]{4,3,2,1,0:T(8,128)(2,1)S(1)}, bf16[1,2,8,64,128]{4,3,2,1,0:T(8,128)(2,1)S(1)}, u32[]{:S(2)}, u32[]{:S(2)}) collective-permute-start(bf16[1,2,8,64,128]{4,3,2,1,0:T(8,128)(2,1)S(1)} %get-tuple-element.55), channel_id=1, source_target_pairs={{0,12},{4,16},{8,20},{12,24},{16,28},{20,0},{24,4},{28,8},{1,13},{... | collective-permute-start | bytes 786440 | tf_op jit(solution)/shard_map/ppermute | solution.py:358
  224.4 23.0 %collective-permute-start.7 = (bf16[1,2,8,64,128]{4,3,2,1,0:T(8,128)(2,1)S(1)}, bf16[1,2,8,64,128]{4,3,2,1,0:T(8,128)(2,1)S(1)}, u32[]{:S(2)}, u32[]{:S(2)}) collective-permute-start(bf16[1,2,8,64,128]{4,3,2,1,0:T(8,128)(2,1)S(1)} %get-tuple-element.56), channel_id=1, source_target_pairs={{0,16},{4,20},{8,24},{12,28},{16,0},{20,4},{24,8},{28,12},{1,17},{... | collective-permute-start | bytes 786440 | tf_op jit(solution)/shard_map/ppermute | solution.py:358
  224.6 22.9 %collective-permute-start.8 = (bf16[1,2,8,64,128]{4,3,2,1,0:T(8,128)(2,1)S(1)}, bf16[1,2,8,64,128]{4,3,2,1,0:T(8,128)(2,1)S(1)}, u32[]{:S(2)}, u32[]{:S(2)}) collective-permute-start(bf16[1,2,8,64,128]{4,3,2,1,0:T(8,128)(2,1)S(1)} %get-tuple-element.57), channel_id=1, source_target_pairs={{0,20},{4,24},{8,28},{12,0},{16,4},{20,8},{24,12},{28,16},{1,21},{... | collective-permute-start | bytes 786440 | tf_op jit(solution)/shard_map/ppermute | solution.py:358
  224.6 28.0 %collective-permute-start.9 = (bf16[1,2,8,64,128]{4,3,2,1,0:T(8,128)(2,1)S(1)}, bf16[1,2,8,64,128]{4,3,2,1,0:T(8,128)(2,1)S(1)}, u32[]{:S(2)}, u32[]{:S(2)}) collective-permute-start(bf16[1,2,8,64,128]{4,3,2,1,0:T(8,128)(2,1)S(1)} %get-tuple-element.58), channel_id=1, source_target_pairs={{0,24},{4,28},{8,0},{12,4},{16,8},{20,12},{24,16},{28,20},{1,25},{... | collective-permute-start | bytes 786440 | tf_op jit(solution)/shard_map/ppermute | solution.py:358
  224.9 27.8 %collective-permute-start.10 = (bf16[1,2,8,64,128]{4,3,2,1,0:T(8,128)(2,1)S(1)}, bf16[1,2,8,64,128]{4,3,2,1,0:T(8,128)(2,1)S(1)}, u32[]{:S(2)}, u32[]{:S(2)}) collective-permute-start(bf16[1,2,8,64,128]{4,3,2,1,0:T(8,128)(2,1)S(1)} %get-tuple-element.59), channel_id=1, source_target_pairs={{0,28},{4,0},{8,4},{12,8},{16,12},{20,16},{24,20},{28,24},{1,29},{... | collective-permute-start | bytes 786440 | tf_op jit(solution)/shard_map/ppermute | solution.py:358
  (31 other events, 110.0 us)

commit v3 on v2

--- a/solution.py
+++ b/solution.py
@@ -208,7 +208,7 @@
             whole,
         ],
         out_specs=pl.BlockSpec((tiles, 2, 8, block, LANES), lambda i: (0, 0, 0, i, 0)),
-        out_shape=jax.ShapeDtypeStruct((tiles, 2, 8, slots, LANES), jnp.bfloat16),
+        out_shape=pltpu.HBM((tiles, 2, 8, slots, LANES), jnp.bfloat16),
         scratch_shapes=[
             pltpu.VMEM((width, tiles * LANES), jnp.bfloat16),
             pltpu.VMEM((tiles, 2, block * 8, LANES), jnp.float32),
@@ -299,7 +299,7 @@
         grid=(columns // 2,),
         in_specs=[whole] * 5 + [columnwise(boxes, part.shape[3]) for part in parts],
         out_specs=[columnwise(each, slots)] * results,
-        out_shape=[jax.ShapeDtypeStruct((each, 2, columns, slots, LANES), jnp.bfloat16)] * results,
+        out_shape=[pltpu.HBM((each, 2, columns, slots, LANES), jnp.bfloat16)] * results,
         scratch_shapes=[
             pltpu.VMEM((2, parents, 2 * LANES), jnp.bfloat16),
             pltpu.VMEM((8, 2 * FREQ, 2 * LANES), jnp.float32),
@@ -429,9 +429,9 @@
     value = patterns(0, inner_halo, 0, 1)
     value, outer_first = lax.optimization_barrier((value, outer_first))
     first = exchange(pieces_of(value))
-    _, outer_second = send_edge(after(own, value), 1, quarter, half - quarter)
-
-    operator, slot_parent, far_list, _ = lax.optimization_barrier((trans, slot_parent, far_list, value))
+    send, outer_second = send_edge(after(own, value), 1, quarter, half - quarter)
+
+    operator, slot_parent, far_list, _ = lax.optimization_barrier((trans, slot_parent, far_list, send))
     tables = [table_of(operator, side * width + box * share, share, repeat) for side in sides]
     order = parent_order()
     listed = jnp.concatenate([far_list[row] for row in cover_rows()])

time: 257 us -> 255 us (level)
  local copies, waits for them, and re-layouts: 37 us -> 29.2 us
  Pallas kernels: 84.4 us -> 87.6 us
    unnamed x87 -> x71, local copies, waits for them, and re-layouts: 19 us -> 11.3 us
    all_to_all x2, waiting for transfers between devices: 0.09 us -> 6.5 us  [exchange(): return lax.all_to_all(value, 'box', 0, 0, tiled=True)]
    ppermute x4, waiting for transfers between devices: 10.9 us -> 6.44 us  [send_edge(): return (send, lax.ppermute(send, 'dir', (inner, outer)[step]))]
  transfers between devices with their start and end apart: 20 -> 20, of which waited for: 12 -> 14; matrix products, arithmetic and copies ran while one was open for 7% -> 8% of each run, Pallas kernels for 28% -> 29%
where the time goes in v3:
time: 255 us; the launch traced here: 254 us
  Pallas kernels  87.6 us (34%)
  waiting for transfers between devices  71.5 us (28%)
  starting transfers between devices  30.3 us (12%)
  local copies, waits for them, and re-layouts  29.2 us (11%)
  blocking collectives  29.2 us (11%)
  other arithmetic  5.65 us (2%)
    ppermute x14, waiting for transfers between devices, send_apart(): lax.ppermute(pieces[s], 'box', [(i, (i + s) % devices) for i in range(dev...  58.5 us
    pallas_call x2, Pallas kernels, far_field(): pl.pallas_call(functools.partial(far_kernel, count=len(parts)), grid=(col...  38.8 us
    pallas_call x3, Pallas kernels, upsample(): pl.pallas_call(upsample_kernel, grid=(steps,), in_specs=[smem, smem, pl.B...  38.4 us
    all_to_all x1, blocking collectives, exchange(): return lax.all_to_all(value, 'box', 0, 0, tiled=True)  29.2 us
    ppermute x14, starting transfers between devices, send_apart(): lax.ppermute(pieces[s], 'box', [(i, (i + s) % devices) for i in range(dev...  14.5 us
    all_to_all x2, starting transfers between devices, exchange(): return lax.all_to_all(value, 'box', 0, 0, tiled=True)  12.1 us
    unnamed x71, local copies, waits for them, and re-layouts  11.3 us
    dynamic_slice x4, local copies, waits for them, and re-layouts, send_edge(): send = lax.dynamic_slice(source, start, (size * LANES, edge))  11.3 us
  transfers between devices with their start and end apart: 20, of which 14 were waited for; matrix products, arithmetic and copies ran while one was open for 8% of the time, Pallas kernels for 29%

profile of v3, /device:TPU:11, one launch (start us, length us, event | category | flops | bytes accessed | tf_op | source)
XLA Modules:
  0.0 253.7 jit_solution(328946176251174243)
XLA Ops:
  0.0 4.6 %constant_dynamic-slice_fusion.1 = bf16[8192,256]{1,0:T(8,128)(2,1)} fusion(bf16[8192,512]{1,0:T(8,128)(2,1)} %bitcast.16, s32[]{:T(128)S(6)} %select_n.92), kind=kLoop, calls=%fused_computation.40 | loop fusion | bytes 8388612 | tf_op jit(solution)/shard_map/dynamic_slice | solution.py:394
  9.4 3.0 %collective-permute-done.halo = bf16[8192,256]{1,0:T(8,128)(2,1)} collective-permute-done((bf16[8192,256]{1,0:T(8,128)(2,1)}, bf16[8192,256]{1,0:T(8,128)(2,1)}, u32[]{:S(2)}, u32[]{:S(2)}) %collective-permute-start) | collective-permute-done | bytes 4194336 | tf_op jit(solution)/shard_map/ppermute | solution.py:395
  12.4 17.7 %upsample.3 = bf16[8,2,8,64,128]{4,3,2,1,0:T(8,128)(2,1)} custom-call(s32[8,4]{1,0:T(8,128)S(1)} %get-tuple-element.96.places, s32[1]{0:T(128)} %bitcast.3.first, bf16[8192,512]{1,0:T(8,128)(2,1)} %bitcast.18, bf16[8192,256]{1,0:T(8,128)(2,1)} %collective-permute-done.halo, bf16[16,4,128,128]{3,2,1,0:T(8,128)(2,1)S(1)} %copy-done.3, ...), custom_call_target="tpu_custom_call" | custom-call | flops 1 | bytes 8192 | tf_op jit(solution)/shard_map/upsample/pallas_call | solution.py:198
  31.6 5.8 %all-to-all-start.1 = ((bf16[8,2,8,64,128]{4,3,2,1,0:T(8,128)(2,1)}), bf16[8,2,8,64,128]{4,3,2,1,0:T(8,128)(2,1)S(1)}, u32[]{:S(2)}, u32[]{:S(2)}) async-start(bf16[8,2,8,64,128]{4,3,2,1,0:T(8,128)(2,1)} %upsample.3), calls=%async_computation.1 | async-start | bytes 4194304 | tf_op jit(solution)/shard_map/all_to_all | solution.py:351
  38.0 2.3 constant_dynamic-slice_fusion.3
  40.2 1.7 collective-permute-start.2
  43.3 1.9 gather_fusion
  46.6 2.6 %copy-done = f32[2,343,2048]{2,0,1:T(2,128)S(1)} copy-done((f32[2,343,2048]{2,0,1:T(2,128)S(1)}, f32[2,343,2048]{2,0,1:T(2,128)}, u32[]{:S(2)}) %copy-start) | copy-done | bytes 5619736
  55.0 2.4 copy-done.1
  57.4 3.1 %constant_dynamic-slice_fusion.2 = bf16[4096,256]{1,0:T(8,128)(2,1)} fusion(bf16[8192,512]{1,0:T(8,128)(2,1)} %bitcast.20, s32[]{:T(128)S(6)} %select_n.94), kind=kLoop, calls=%fused_computation.46 | loop fusion | bytes 4194308 | tf_op jit(solution)/shard_map/dynamic_slice | solution.py:394
  64.4 1.9 collective-permute-done.2
  66.3 1.7 pad_maximum_fusion.halo
  68.0 10.2 %upsample.4 = bf16[8,2,8,32,128]{4,3,2,1,0:T(8,128)(2,1)} custom-call(s32[8,4]{1,0:T(8,128)S(1)} %copy-done.17, s32[1]{0:T(128)} %bitcast.7.first, bf16[8192,512]{1,0:T(8,128)(2,1)} %bitcast.21, bf16[4096,256]{1,0:T(8,128)(2,1)S(1)} %pad_maximum_fusion.halo, bf16[16,4,128,128]{3,2,1,0:T(8,128)(2,1)S(1)} %copy-done.4, f32[8,1024]{1,0:T(8,128)S(1)} %copy-done.16, ...), custom_call_target="tpu_custom_call" | custom-call | flops 12000000000 | bytes 4096 | tf_op jit(solution)/shard_map/upsample/pallas_call | solution.py:198
  78.2 4.9 %all-to-all-done.1.rest_0_ = bf16[8,2,8,64,128]{4,3,2,1,0:T(8,128)(2,1)S(1)} async-done(((bf16[8,2,8,64,128]{4,3,2,1,0:T(8,128)(2,1)}), bf16[8,2,8,64,128]{4,3,2,1,0:T(8,128)(2,1)S(1)}, u32[]{:S(2)}, u32[]{:S(2)}) %all-to-all-start.1) | async-done | bytes 2097184 | tf_op jit(solution)/shard_map/all_to_all | solution.py:351
  83.1 6.3 %all-to-all-start = ((bf16[8,2,8,32,128]{4,3,2,1,0:T(8,128)(2,1)}), bf16[8,2,8,32,128]{4,3,2,1,0:T(8,128)(2,1)S(1)}, u32[]{:S(2)}, u32[]{:S(2)}) async-start(bf16[8,2,8,32,128]{4,3,2,1,0:T(8,128)(2,1)} %upsample.4), calls=%async_computation | async-start | bytes 2097152 | tf_op jit(solution)/shard_map/all_to_all | solution.py:351
  91.5 19.4 %far_field.2 = (bf16[1,2,8,64,128]{4,3,2,1,0:T(8,128)(2,1)}, bf16[1,2,8,64,128]{4,3,2,1,0:T(8,128)(2,1)}, bf16[1,2,8,64,128]{4,3,2,1,0:T(8,128)(2,1)}, bf16[1,2,...) custom-call(bf16[512,512]{1,0:T(8,128)(2,1)S(1)} %copy-done.12, ...), custom_call_target="tpu_custom_call" | custom-call | flops 20000000000 | bytes 12582912 | tf_op jit(solution)/shard_map/far_field/pallas_call | solution.py:297
  114.3 10.5 %upsample.5 = bf16[8,2,8,32,128]{4,3,2,1,0:T(8,128)(2,1)} custom-call(s32[8,4]{1,0:T(8,128)S(1)} %copy-done.17, s32[1]{0:T(128)} %bitcast.7.first, bf16[8192,512]{1,0:T(8,128)(2,1)} %bitcast.22, bf16[4096,256]{1,0:T(8,128)(2,1)} %collective-permute-done.3.halo, bf16[16,4,128,128]{3,2,1,0:T(8,128)(2,1)S(1)} %copy-done.5, f32[8,1024]{1,0:T(8,128)S(1)} %copy-done.16, ...), custom_call_target="tpu_custom_call" | custom-call | flops 12000000000 | bytes 4096 | tf_op jit(solution)/shard_map/upsample/pallas_call | solution.py:198
  124.8 29.2 %all_to_all.15.rest_1_ = bf16[8,2,8,32,128]{4,3,2,1,0:T(8,128)(2,1)S(1)} all-to-all(bf16[8,2,8,32,128]{4,3,2,1,0:T(8,128)(2,1)} %upsample.5), channel_id=1, replica_groups=mesh['box'=8,'dir'=4] {'box'}, dimensions={0} | all-to-all | bytes 2097152 | tf_op jit(solution)/shard_map/all_to_all | solution.py:351
  154.1 2.1 collective-permute-start.11
  157.0 2.5 collective-permute-start.13
  159.5 19.4 %far_field.3 = (bf16[1,2,8,64,128]{4,3,2,1,0:T(8,128)(2,1)}, bf16[1,2,8,64,128]{4,3,2,1,0:T(8,128)(2,1)}, bf16[1,2,8,64,128]{4,3,2,1,0:T(8,128)(2,1)}, bf16[1,2,...) custom-call(bf16[512,512]{1,0:T(8,128)(2,1)S(1)} %copy-done.13, ...), custom_call_target="tpu_custom_call" | custom-call | flops 20000000000 | bytes 12582912 | tf_op jit(solution)/shard_map/far_field/pallas_call | solution.py:297
  179.0 1.7 collective-permute-start.15
  180.6 1.7 collective-permute-start.16
  182.7 1.9 collective-permute-start.4
  184.7 15.0 %collective-permute-done.14.rest_4_ = bf16[1,2,8,64,128]{4,3,2,1,0:T(8,128)(2,1)S(1)} collective-permute-done((bf16[1,2,8,64,128]{4,3,2,1,0:T(8,128)(2,1)S(1)}, bf16[1,2,8,64,128]{4,3,2,1,0:T(8,128)(2,1)S(1)}, u32[]{:S(2)}, u32[]{:S(2)}) %collective-permute-start.14) | collective-permute-done | bytes 262176 | tf_op jit(solution)/shard_map/ppermute | solution.py:358
  199.7 3.5 %collective-permute-done.15.rest_5_ = bf16[1,2,8,64,128]{4,3,2,1,0:T(8,128)(2,1)S(1)} collective-permute-done((bf16[1,2,8,64,128]{4,3,2,1,0:T(8,128)(2,1)S(1)}, bf16[1,2,8,64,128]{4,3,2,1,0:T(8,128)(2,1)S(1)}, u32[]{:S(2)}, u32[]{:S(2)}) %collective-permute-start.15) | collective-permute-done | bytes 262176 | tf_op jit(solution)/shard_map/ppermute | solution.py:358
  203.2 18.7 %collective-permute-done.16.rest_6_ = bf16[1,2,8,64,128]{4,3,2,1,0:T(8,128)(2,1)S(1)} collective-permute-done((bf16[1,2,8,64,128]{4,3,2,1,0:T(8,128)(2,1)S(1)}, bf16[1,2,8,64,128]{4,3,2,1,0:T(8,128)(2,1)S(1)}, u32[]{:S(2)}, u32[]{:S(2)}) %collective-permute-start.16) | collective-permute-done | bytes 262176 | tf_op jit(solution)/shard_map/ppermute | solution.py:358
  222.5 3.1 %collective-permute-start.10 = (bf16[1,2,8,64,128]{4,3,2,1,0:T(8,128)(2,1)}, bf16[1,2,8,64,128]{4,3,2,1,0:T(8,128)(2,1)S(1)}, u32[]{:S(2)}, u32[]{:S(2)}) collective-permute-start(bf16[1,2,8,64,128]{4,3,2,1,0:T(8,128)(2,1)} %get-tuple-element.59), channel_id=1, source_target_pairs={{0,28},{4,0},{8,4},{12,8},{16,12},{20,16},{24,20},{28,24},{1,29},{... | collective-permute-start | bytes 786440 | tf_op jit(solution)/shard_map/ppermute | solution.py:358
  225.6 3.5 %finish.2.rest_8_ = f32[1024,2048]{1,0:T(8,128)} custom-call(s32[1]{0:T(128)} %bitcast.9.side, s32[1]{0:T(128)} %bitcast.1.me, bf16[1,2,8,64,128]{4,3,2,1,0:T(8,128)(2,1)S(1)} %copy-done.15, bf16[1,2,8,64,128]{4,3,2,1,0:T(8,128)(2,1)S(1)} %collective-permute-done.11.rest_1_, bf16[1,2,8,64,128]{4,3,2,1,0:T(8,128)(2,1)S(1)} %collective-permute-done.12.rest_2_, ...), custom_call_target="tpu_custom_call" | custom-call | tf_op jit(solution)/shard_map/finish/pallas_call | solution.py:333
  229.1 16.2 %collective-permute-done.7.rest_4_ = bf16[1,2,8,64,128]{4,3,2,1,0:T(8,128)(2,1)S(1)} collective-permute-done((bf16[1,2,8,64,128]{4,3,2,1,0:T(8,128)(2,1)}, bf16[1,2,8,64,128]{4,3,2,1,0:T(8,128)(2,1)S(1)}, u32[]{:S(2)}, u32[]{:S(2)}) %collective-permute-start.7) | collective-permute-done | bytes 262176 | tf_op jit(solution)/shard_map/ppermute | solution.py:358
  245.3 4.8 %collective-permute-done.9.rest_6_ = bf16[1,2,8,64,128]{4,3,2,1,0:T(8,128)(2,1)S(1)} collective-permute-done((bf16[1,2,8,64,128]{4,3,2,1,0:T(8,128)(2,1)}, bf16[1,2,8,64,128]{4,3,2,1,0:T(8,128)(2,1)S(1)}, u32[]{:S(2)}, u32[]{:S(2)}) %collective-permute-start.9) | collective-permute-done | bytes 262176 | tf_op jit(solution)/shard_map/ppermute | solution.py:358
  250.2 3.5 %finish.3 = f32[1024,2048]{1,0:T(8,128)} custom-call(s32[1]{0:T(128)} %bitcast.side, s32[1]{0:T(128)} %bitcast.1.me, bf16[1,2,8,64,128]{4,3,2,1,0:T(8,128)(2,1)S(1)} %copy-done.14, bf16[1,2,8,64,128]{4,3,2,1,0:T(8,128)(2,1)S(1)} %collective-permute-done.4.rest_1_, ...), custom_call_target="tpu_custom_call", output_to_operand_aliasing={{}: (10, {})} | custom-call | tf_op jit(solution)/shard_map/finish/pallas_call | solution.py:333
  (108 shorter events, 26.5 us)
Async XLA Ops:
  4.6 7.8 %collective-permute-start = (bf16[8192,256]{1,0:T(8,128)(2,1)}, bf16[8192,256]{1,0:T(8,128)(2,1)}, u32[]{:S(2)}, u32[]{:S(2)}) collective-permute-start(bf16[8192,256]{1,0:T(8,128)(2,1)} %constant_dynamic-slice_fusion.1), channel_id=1, source_target_pairs={{0,1},{1,0},{2,3},{3,2},{4,5},{5,4},{6,7},{7,6},{8,9},{9,8},{10,11... | collective-permute-start | bytes 12582920 | tf_op jit(solution)/shard_map/ppermute | solution.py:395
  6.6 24.9 %collective-permute-start.1 = (bf16[2048,256]{1,0:T(8,128)(2,1)S(1)}, bf16[2048,256]{1,0:T(8,128)(2,1)}, u32[]{:S(2)}, u32[]{:S(2)}) collective-permute-start(bf16[2048,256]{1,0:T(8,128)(2,1)S(1)} %constant_dynamic-slice_fusion), channel_id=1, source_target_pairs={{0,3},{1,2},{2,1},{3,0},{4,7},{5,6},{6,5},{7,4},{8,11},{9,10},{10,... | collective-permute-start | bytes 3145736 | tf_op jit(solution)/shard_map/ppermute | solution.py:395
  31.6 51.5 %all-to-all-start.1 = ((bf16[8,2,8,64,128]{4,3,2,1,0:T(8,128)(2,1)}), bf16[8,2,8,64,128]{4,3,2,1,0:T(8,128)(2,1)S(1)}, u32[]{:S(2)}, u32[]{:S(2)}) async-start(bf16[8,2,8,64,128]{4,3,2,1,0:T(8,128)(2,1)} %upsample.3), calls=%async_computation.1 | async-start | bytes 4194304 | tf_op jit(solution)/shard_map/all_to_all | solution.py:351
  40.2 26.1 %collective-permute-start.2 = (bf16[2048,256]{1,0:T(8,128)(2,1)}, bf16[2048,256]{1,0:T(8,128)(2,1)}, u32[]{:S(2)}, u32[]{:S(2)}) collective-permute-start(bf16[2048,256]{1,0:T(8,128)(2,1)} %constant_dynamic-slice_fusion.3), channel_id=1, source_target_pairs={{0,3},{1,2},{2,1},{3,0},{4,7},{5,6},{6,5},{7,4},{8,11},{9,10},{10,... | collective-permute-start | bytes 3145736 | tf_op jit(solution)/shard_map/ppermute | solution.py:395
  60.5 50.6 %collective-permute-start.3 = (bf16[4096,256]{1,0:T(8,128)(2,1)}, bf16[4096,256]{1,0:T(8,128)(2,1)}, u32[]{:S(2)}, u32[]{:S(2)}) collective-permute-start(bf16[4096,256]{1,0:T(8,128)(2,1)} %constant_dynamic-slice_fusion.2), channel_id=1, source_target_pairs={{0,3},{1,2},{2,1},{3,0},{4,7},{5,6},{6,5},{7,4},{8,11},{9,10},{10,... | collective-permute-start | bytes 6291464 | tf_op jit(solution)/shard_map/ppermute | solution.py:395
  68.0 21.4 %copy-start.18 = (bf16[128,768]{1,0:T(8,128)(2,1)S(1)}, bf16[128,768]{1,0:T(8,128)(2,1)}, u32[]{:S(2)}) copy-start(bf16[128,768]{1,0:T(8,128)(2,1)} %constant.130.clone.inverse) | copy-start | bytes 589828
  83.1 29.6 %all-to-all-start = ((bf16[8,2,8,32,128]{4,3,2,1,0:T(8,128)(2,1)}), bf16[8,2,8,32,128]{4,3,2,1,0:T(8,128)(2,1)S(1)}, u32[]{:S(2)}, u32[]{:S(2)}) async-start(bf16[8,2,8,32,128]{4,3,2,1,0:T(8,128)(2,1)} %upsample.4), calls=%async_computation | async-start | bytes 2097152 | tf_op jit(solution)/shard_map/all_to_all | solution.py:351
  114.3 39.8 %copy-start.32 = (bf16[1,2,8,64,128]{4,3,2,1,0:T(8,128)(2,1)S(1)}, bf16[1,2,8,64,128]{4,3,2,1,0:T(8,128)(2,1)}, u32[]{:S(2)}) copy-start(bf16[1,2,8,64,128]{4,3,2,1,0:T(8,128)(2,1)} %get-tuple-element.62) | copy-start | bytes 786436
  114.3 41.9 %copy-start.31 = (bf16[1,2,8,64,128]{4,3,2,1,0:T(8,128)(2,1)S(1)}, bf16[1,2,8,64,128]{4,3,2,1,0:T(8,128)(2,1)}, u32[]{:S(2)}) copy-start(bf16[1,2,8,64,128]{4,3,2,1,0:T(8,128)(2,1)} %get-tuple-element.64) | copy-start | bytes 786436
  114.3 42.7 %copy-start.30 = (bf16[1,2,8,64,128]{4,3,2,1,0:T(8,128)(2,1)S(1)}, bf16[1,2,8,64,128]{4,3,2,1,0:T(8,128)(2,1)}, u32[]{:S(2)}) copy-start(bf16[1,2,8,64,128]{4,3,2,1,0:T(8,128)(2,1)} %get-tuple-element.66) | copy-start | bytes 786436
  114.3 45.2 %copy-start.29 = (bf16[1,2,8,64,128]{4,3,2,1,0:T(8,128)(2,1)S(1)}, bf16[1,2,8,64,128]{4,3,2,1,0:T(8,128)(2,1)}, u32[]{:S(2)}) copy-start(bf16[1,2,8,64,128]{4,3,2,1,0:T(8,128)(2,1)} %get-tuple-element.68) | copy-start | bytes 786436
  114.3 45.2 %copy-start.11 = (bf16[512,512]{1,0:T(8,128)(2,1)S(1)}, bf16[512,512]{1,0:T(8,128)(2,1)}, u32[]{:S(2)}) copy-start(bf16[512,512]{1,0:T(8,128)(2,1)} %get-tuple-element.97.back) | copy-start | bytes 1572868
  114.3 45.2 %copy-start.13 = (bf16[512,512]{1,0:T(8,128)(2,1)S(1)}, bf16[512,512]{1,0:T(8,128)(2,1)}, u32[]{:S(2)}) copy-start(bf16[512,512]{1,0:T(8,128)(2,1)} %get-tuple-element.98.into) | copy-start | bytes 1572868
  154.1 24.9 %copy-start.28 = (bf16[1,2,8,64,128]{4,3,2,1,0:T(8,128)(2,1)S(1)}, bf16[1,2,8,64,128]{4,3,2,1,0:T(8,128)(2,1)}, u32[]{:S(2)}) copy-start(bf16[1,2,8,64,128]{4,3,2,1,0:T(8,128)(2,1)} %get-tuple-element.70) | copy-start | bytes 786436
  154.1 26.6 %copy-start.27 = (bf16[1,2,8,64,128]{4,3,2,1,0:T(8,128)(2,1)S(1)}, bf16[1,2,8,64,128]{4,3,2,1,0:T(8,128)(2,1)}, u32[]{:S(2)}) copy-start(bf16[1,2,8,64,128]{4,3,2,1,0:T(8,128)(2,1)} %get-tuple-element.72) | copy-start | bytes 786436
  154.1 28.2 %copy-start.26 = (bf16[1,2,8,64,128]{4,3,2,1,0:T(8,128)(2,1)S(1)}, bf16[1,2,8,64,128]{4,3,2,1,0:T(8,128)(2,1)}, u32[]{:S(2)}) copy-start(bf16[1,2,8,64,128]{4,3,2,1,0:T(8,128)(2,1)} %get-tuple-element.74) | copy-start | bytes 786436
  154.1 71.5 %copy-start.15 = (bf16[1,2,8,64,128]{4,3,2,1,0:T(8,128)(2,1)S(1)}, bf16[1,2,8,64,128]{4,3,2,1,0:T(8,128)(2,1)}, u32[]{:S(2)}) copy-start(bf16[1,2,8,64,128]{4,3,2,1,0:T(8,128)(2,1)} %get-tuple-element.60.rest_0_) | copy-start | bytes 786436
  154.1 26.5 %collective-permute-start.11 = (bf16[1,2,8,64,128]{4,3,2,1,0:T(8,128)(2,1)S(1)}, bf16[1,2,8,64,128]{4,3,2,1,0:T(8,128)(2,1)S(1)}, u32[]{:S(2)}, u32[]{:S(2)}) collective-permute-start(bf16[1,2,8,64,128]{4,3,2,1,0:T(8,128)(2,1)S(1)} %copy-done.32), channel_id=1, source_target_pairs={{0,4},{4,8},{8,12},{12,16},{16,20},{20,24},{24,28},{28,0},{1,5},{5... | collective-permute-start | bytes 786440 | tf_op jit(solution)/shard_map/ppermute | solution.py:358
  156.1 26.2 %collective-permute-start.12 = (bf16[1,2,8,64,128]{4,3,2,1,0:T(8,128)(2,1)S(1)}, bf16[1,2,8,64,128]{4,3,2,1,0:T(8,128)(2,1)S(1)}, u32[]{:S(2)}, u32[]{:S(2)}) collective-permute-start(bf16[1,2,8,64,128]{4,3,2,1,0:T(8,128)(2,1)S(1)} %copy-done.31), channel_id=1, source_target_pairs={{0,8},{4,12},{8,16},{12,20},{16,24},{20,28},{24,0},{28,4},{1,9},{5... | collective-permute-start | bytes 786440 | tf_op jit(solution)/shard_map/ppermute | solution.py:358
  157.0 25.7 %collective-permute-start.13 = (bf16[1,2,8,64,128]{4,3,2,1,0:T(8,128)(2,1)S(1)}, bf16[1,2,8,64,128]{4,3,2,1,0:T(8,128)(2,1)S(1)}, u32[]{:S(2)}, u32[]{:S(2)}) collective-permute-start(bf16[1,2,8,64,128]{4,3,2,1,0:T(8,128)(2,1)S(1)} %copy-done.30), channel_id=1, source_target_pairs={{0,12},{4,16},{8,20},{12,24},{16,28},{20,0},{24,4},{28,8},{1,13},{... | collective-permute-start | bytes 786440 | tf_op jit(solution)/shard_map/ppermute | solution.py:358
  159.5 40.2 %collective-permute-start.14 = (bf16[1,2,8,64,128]{4,3,2,1,0:T(8,128)(2,1)S(1)}, bf16[1,2,8,64,128]{4,3,2,1,0:T(8,128)(2,1)S(1)}, u32[]{:S(2)}, u32[]{:S(2)}) collective-permute-start(bf16[1,2,8,64,128]{4,3,2,1,0:T(8,128)(2,1)S(1)} %copy-done.29), channel_id=1, source_target_pairs={{0,16},{4,20},{8,24},{12,28},{16,0},{20,4},{24,8},{28,12},{1,17},{... | collective-permute-start | bytes 786440 | tf_op jit(solution)/shard_map/ppermute | solution.py:358
  179.0 24.2 %collective-permute-start.15 = (bf16[1,2,8,64,128]{4,3,2,1,0:T(8,128)(2,1)S(1)}, bf16[1,2,8,64,128]{4,3,2,1,0:T(8,128)(2,1)S(1)}, u32[]{:S(2)}, u32[]{:S(2)}) collective-permute-start(bf16[1,2,8,64,128]{4,3,2,1,0:T(8,128)(2,1)S(1)} %copy-done.28), channel_id=1, source_target_pairs={{0,20},{4,24},{8,28},{12,0},{16,4},{20,8},{24,12},{28,16},{1,21},{... | collective-permute-start | bytes 786440 | tf_op jit(solution)/shard_map/ppermute | solution.py:358
  180.6 41.3 %collective-permute-start.16 = (bf16[1,2,8,64,128]{4,3,2,1,0:T(8,128)(2,1)S(1)}, bf16[1,2,8,64,128]{4,3,2,1,0:T(8,128)(2,1)S(1)}, u32[]{:S(2)}, u32[]{:S(2)}) collective-permute-start(bf16[1,2,8,64,128]{4,3,2,1,0:T(8,128)(2,1)S(1)} %copy-done.27), channel_id=1, source_target_pairs={{0,24},{4,28},{8,0},{12,4},{16,8},{20,12},{24,16},{28,20},{1,25},{... | collective-permute-start | bytes 786440 | tf_op jit(solution)/shard_map/ppermute | solution.py:358
  182.3 39.7 %collective-permute-start.17 = (bf16[1,2,8,64,128]{4,3,2,1,0:T(8,128)(2,1)S(1)}, bf16[1,2,8,64,128]{4,3,2,1,0:T(8,128)(2,1)S(1)}, u32[]{:S(2)}, u32[]{:S(2)}) collective-permute-start(bf16[1,2,8,64,128]{4,3,2,1,0:T(8,128)(2,1)S(1)} %copy-done.26), channel_id=1, source_target_pairs={{0,28},{4,0},{8,4},{12,8},{16,12},{20,16},{24,20},{28,24},{1,29},{... | collective-permute-start | bytes 786440 | tf_op jit(solution)/shard_map/ppermute | solution.py:358
  182.7 39.3 %collective-permute-start.4 = (bf16[1,2,8,64,128]{4,3,2,1,0:T(8,128)(2,1)}, bf16[1,2,8,64,128]{4,3,2,1,0:T(8,128)(2,1)S(1)}, u32[]{:S(2)}, u32[]{:S(2)}) collective-permute-start(bf16[1,2,8,64,128]{4,3,2,1,0:T(8,128)(2,1)} %get-tuple-element.53), channel_id=1, source_target_pairs={{0,4},{4,8},{8,12},{12,16},{16,20},{20,24},{24,28},{28,0},{1,5},{5... | collective-permute-start | bytes 786440 | tf_op jit(solution)/shard_map/ppermute | solution.py:358
  199.7 22.7 %collective-permute-start.5 = (bf16[1,2,8,64,128]{4,3,2,1,0:T(8,128)(2,1)}, bf16[1,2,8,64,128]{4,3,2,1,0:T(8,128)(2,1)S(1)}, u32[]{:S(2)}, u32[]{:S(2)}) collective-permute-start(bf16[1,2,8,64,128]{4,3,2,1,0:T(8,128)(2,1)} %get-tuple-element.54), channel_id=1, source_target_pairs={{0,8},{4,12},{8,16},{12,20},{16,24},{20,28},{24,0},{28,4},{1,9},{5... | collective-permute-start | bytes 786440 | tf_op jit(solution)/shard_map/ppermute | solution.py:358
  203.2 25.9 %collective-permute-start.6 = (bf16[1,2,8,64,128]{4,3,2,1,0:T(8,128)(2,1)}, bf16[1,2,8,64,128]{4,3,2,1,0:T(8,128)(2,1)S(1)}, u32[]{:S(2)}, u32[]{:S(2)}) collective-permute-start(bf16[1,2,8,64,128]{4,3,2,1,0:T(8,128)(2,1)} %get-tuple-element.55), channel_id=1, source_target_pairs={{0,12},{4,16},{8,20},{12,24},{16,28},{20,0},{24,4},{28,8},{1,13},{... | collective-permute-start | bytes 786440 | tf_op jit(solution)/shard_map/ppermute | solution.py:358
  221.9 23.4 %collective-permute-start.7 = (bf16[1,2,8,64,128]{4,3,2,1,0:T(8,128)(2,1)}, bf16[1,2,8,64,128]{4,3,2,1,0:T(8,128)(2,1)S(1)}, u32[]{:S(2)}, u32[]{:S(2)}) collective-permute-start(bf16[1,2,8,64,128]{4,3,2,1,0:T(8,128)(2,1)} %get-tuple-element.56), channel_id=1, source_target_pairs={{0,16},{4,20},{8,24},{12,28},{16,0},{20,4},{24,8},{28,12},{1,17},{... | collective-permute-start | bytes 786440 | tf_op jit(solution)/shard_map/ppermute | solution.py:358
  222.0 23.3 %collective-permute-start.8 = (bf16[1,2,8,64,128]{4,3,2,1,0:T(8,128)(2,1)}, bf16[1,2,8,64,128]{4,3,2,1,0:T(8,128)(2,1)S(1)}, u32[]{:S(2)}, u32[]{:S(2)}) collective-permute-start(bf16[1,2,8,64,128]{4,3,2,1,0:T(8,128)(2,1)} %get-tuple-element.57), channel_id=1, source_target_pairs={{0,20},{4,24},{8,28},{12,0},{16,4},{20,8},{24,12},{28,16},{1,21},{... | collective-permute-start | bytes 786440 | tf_op jit(solution)/shard_map/ppermute | solution.py:358
  222.0 28.1 %collective-permute-start.9 = (bf16[1,2,8,64,128]{4,3,2,1,0:T(8,128)(2,1)}, bf16[1,2,8,64,128]{4,3,2,1,0:T(8,128)(2,1)S(1)}, u32[]{:S(2)}, u32[]{:S(2)}) collective-permute-start(bf16[1,2,8,64,128]{4,3,2,1,0:T(8,128)(2,1)} %get-tuple-element.58), channel_id=1, source_target_pairs={{0,24},{4,28},{8,0},{12,4},{16,8},{20,12},{24,16},{28,20},{1,25},{... | collective-permute-start | bytes 786440 | tf_op jit(solution)/shard_map/ppermute | solution.py:358
  222.5 27.7 %collective-permute-start.10 = (bf16[1,2,8,64,128]{4,3,2,1,0:T(8,128)(2,1)}, bf16[1,2,8,64,128]{4,3,2,1,0:T(8,128)(2,1)S(1)}, u32[]{:S(2)}, u32[]{:S(2)}) collective-permute-start(bf16[1,2,8,64,128]{4,3,2,1,0:T(8,128)(2,1)} %get-tuple-element.59), channel_id=1, source_target_pairs={{0,28},{4,0},{8,4},{12,8},{16,12},{20,16},{24,20},{28,24},{1,29},{... | collective-permute-start | bytes 786440 | tf_op jit(solution)/shard_map/ppermute | solution.py:358
  225.6 24.6 %copy-start.14 = (bf16[1,2,8,64,128]{4,3,2,1,0:T(8,128)(2,1)S(1)}, bf16[1,2,8,64,128]{4,3,2,1,0:T(8,128)(2,1)}, u32[]{:S(2)}) copy-start(bf16[1,2,8,64,128]{4,3,2,1,0:T(8,128)(2,1)} %get-tuple-element.52.rest_0_) | copy-start | bytes 786436
  (23 other events, 130.9 us)
